TPU v7x, 32 devices: a whole 2x2x4 slice. The times are simulated.
32 devices in a mesh: groups: 2 (over x), fsdp: 16 (over z, y, core).
Axes of the slice: x: 2, y: 2, z: 4, core: 2. Of those that a mesh axis runs over, the one named last changes fastest.
Arguments:
- expert_grad: float32 [8, 3, 768, 2048], P('groups', None, 'fsdp'), parts along dimension 0, may hold values from -12 to 12
- expert_momentum: float32 [8, 3, 768, 2048], P('groups', None, 'fsdp'), parts along dimension 0, may hold values from -6 to 6
- expert_master: float32 [8, 3, 768, 2048], P('groups', None, 'fsdp'), parts along dimension 0, may hold values from -6 to 6
- kv_grad: float32 [4, 512, 2048], P('groups', 'fsdp'), parts along dimension 0, may hold values from -12 to 12
- kv_momentum: float32 [4, 512, 2048], P('groups', 'fsdp'), parts along dimension 0, may hold values from -6 to 6
- kv_master: float32 [4, 512, 2048], P('groups', 'fsdp'), parts along dimension 0, may hold values from -6 to 6
Outputs:
- expert_master_new: float32 [8, 3, 768, 2048], P('groups', None, 'fsdp'), parts along dimension 0
- expert_momentum_new: float32 [8, 3, 768, 2048], P('groups', None, 'fsdp'), parts along dimension 0
- expert_weights: bfloat16 [8, 3, 768, 2048], P('groups', None, 'fsdp'), parts along dimension 0
- expert_update: bfloat16 [8, 3, 768, 2048], P('groups', None, 'fsdp'), parts along dimension 0
- kv_master_new: float32 [4, 512, 2048], P('groups', 'fsdp'), parts along dimension 0
- kv_momentum_new: float32 [4, 512, 2048], P('groups', 'fsdp'), parts along dimension 0
- kv_weights: bfloat16 [4, 512, 2048], P('groups', 'fsdp'), parts along dimension 0
- kv_update: bfloat16 [4, 512, 2048], P('groups', 'fsdp'), parts along dimension 0
There are 2 independent parts, one for each index of `groups`. A program takes and returns all parts, laid end to end along the dimension named above; each array names one. Nothing has to cross between parts.
All inputs are finite; a program needn't handle non-finite values.
Results may differ from a plain program's by a relative error of at most 0.014.
Values may be sent and summed in bfloat16 or wider, within the bound.
No kernel may reach another device: no remote copies, remote signals or barrier semaphores. Data moves between devices by JAX's collectives and lax.ppermute only.
A program may use at most 128 MiB of HBM per device.

v0:
```python
import functools
import math

import jax
import jax.numpy as jnp
import numpy as np
from jax import lax
from jax.experimental import pallas as pl
from jax.experimental.pallas import tpu as pltpu
from jax.sharding import PartitionSpec as P

NS_A = 3.4445
NS_B = -4.775
NS_C = 2.0315
MOMENTUM = 0.95
RATE = 0.02
DECAY = 0.1
NORM_EPS = 1e-07
CLIP_EPS = 1e-06
CLIP_RATIO = 0.5
UPDATE_GAIN = 0.2

F32 = jnp.float32
BF16 = jnp.bfloat16
VMEM_LIMIT = 40 * 1024 * 1024
LOAD_LIMIT = 42 * 1024 * 1024
STREAM_LIMIT = 16 * 1024 * 1024


def owner_table(experts, kvs, devices):
    table = np.zeros((2, devices), np.int32)
    chips = devices // 2
    first = min(experts, chips)
    for index in range(first):
        table[:, 2 * (index * chips // first)] = (1, index)
    by_parity = sorted(range(chips), key=lambda chip: bin(chip).count("1") % 2)
    for index in range(first, experts):
        table[:, 2 * by_parity[index - first] + 1] = (1, index)
    for index in range(kvs):
        low = index * devices // kvs
        free = [d for d in range(low, low + devices // kvs) if d % 2 and not table[0, d]]
        table[:, free[0]] = (2, index)
    return table


def near_owners(devices, flip):
    chips = devices // 4
    return [
        [2 * (device // (2 * chips) * chips + chip) + (device % 2 ^ flip) for chip in range(chips)]
        for device in range(devices)
    ]


def far_owners(devices, flip):
    steps = range(devices // 4, devices // 2)
    return [[device ^ (2 * step) ^ flip for step in steps] for device in range(devices)]


def visit_tables(table, owners):
    kinds = np.zeros((len(owners), len(owners[0])), np.int32)
    held = np.zeros_like(kinds)
    for device, row in enumerate(owners):
        experts = [table[1, owner] for owner in row if table[0, owner] == 1]
        last = experts[0] if experts else 0
        for place, owner in enumerate(row):
            kinds[device, place] = table[0, owner]
            last = table[1, owner] if table[0, owner] == 1 else last
            held[device, place] = last
    return kinds, held


def visits(table, owners):
    return tuple(jnp.asarray(part.reshape(-1)) for part in visit_tables(table, owners))


def joined(*parts):
    return [sum(rows, []) for rows in zip(*parts)]


def load_kernel(eg, em, kg, km, partial, gv, mv, kgv, kmv, total, sems, kv_sems):
    chunks = sems.shape[1]
    size = gv.shape[0] // chunks
    copies = [
        [
            pltpu.make_async_copy(
                source.at[pl.ds(chunk * size, size)],
                target.at[pl.ds(chunk * size, size)],
                sems.at[place, chunk],
            )
            for chunk in range(chunks)
        ]
        for place, (source, target) in enumerate(((eg, gv), (em, mv)))
    ]
    kv_copies = [
        pltpu.make_async_copy(source, target, kv_sems.at[place])
        for place, (source, target) in enumerate(((kg, kgv), (km, kmv)))
    ]
    for copy in kv_copies + copies[0] + copies[1]:
        copy.start()

    def fold(block):
        rows = block.reshape(-1, total.shape[0], block.shape[-1])
        return jnp.sum(rows * rows, axis=0)

    kv_copies[0].wait()
    total[...] = fold(kgv[...])
    for chunk in range(chunks):
        copies[0][chunk].wait()
        total[...] += fold(gv[chunk * size : (chunk + 1) * size])
    partial[...] = jnp.full(partial.shape, jnp.sum(total[...]), F32)
    kv_copies[1].wait()
    for copy in copies[1]:
        copy.wait()


def load(eg, em, kg, km, devices):
    vmem = pl.BlockSpec(memory_space=pltpu.VMEM)
    hbm = pl.BlockSpec(memory_space=pltpu.HBM)
    chunks = eg.shape[0] // 3
    rows = math.gcd(8, 3 * eg.shape[1], kg.shape[1])
    return pl.pallas_call(
        load_kernel,
        in_specs=[hbm] * 4,
        out_specs=[vmem] * 5,
        out_shape=[jax.ShapeDtypeStruct((devices, 8, 128), F32)]
        + [jax.ShapeDtypeStruct(array.shape, F32) for array in (eg, em, kg, km)],
        scratch_shapes=[
            pltpu.VMEM((rows, eg.shape[2]), F32),
            pltpu.SemaphoreType.DMA((2, chunks)),
            pltpu.SemaphoreType.DMA((2,)),
        ],
        compiler_params=pltpu.CompilerParams(vmem_limit_bytes=LOAD_LIMIT),
        name="load",
    )(eg, em, kg, km)


def stage_kernel(devices, me, held, gv, mv, kg, km, staged, keep, away):
    mine = (me[0] >= devices // 2).astype(jnp.int32)
    for out, index in ((keep, mine), (away, 1 - mine)):
        out[0] = kg[index].astype(BF16)
        out[1] = km[index].astype(BF16)
    chips = staged.shape[1]
    for step in range(chips):
        expert = held[me[0] * chips + step]
        staged[0, step] = gv[expert].astype(BF16)
        staged[1, step] = mv[expert].astype(BF16)


def stage(me, table, gv, mv, kg, km):
    _, rows, width = gv.shape
    devices = table.shape[1]
    _, held = visits(table, joined(near_owners(devices, 1), far_owners(devices, 1)))
    vmem = pl.BlockSpec(memory_space=pltpu.VMEM)
    smem = pl.BlockSpec(memory_space=pltpu.SMEM)
    kv = jax.ShapeDtypeStruct((2,) + kg.shape[1:], BF16)
    return pl.pallas_call(
        functools.partial(stage_kernel, devices),
        in_specs=[smem] * 2 + [vmem] * 4,
        out_specs=[vmem] * 3,
        out_shape=[jax.ShapeDtypeStruct((2, devices // 2, rows, width), BF16), kv, kv],
        compiler_params=pltpu.CompilerParams(vmem_limit_bytes=STREAM_LIMIT),
        name="stage",
    )(me, held, gv, mv, kg, km)


def nesterov(scale, grad, moment):
    clipped = scale * grad.astype(F32)
    return (clipped + MOMENTUM * (MOMENTUM * moment.astype(F32) + clipped)).astype(BF16)


def form_far_kernel(count, start, me, kinds, index, squares, gv, mv, sib, clip, *outs):
    total = jnp.sum(squares[...], axis=0)
    factor = jnp.minimum(1.0, count / (jnp.sqrt(total) + CLIP_EPS))
    clip[...] = factor
    scale = factor[0:1, 0:1]
    for step, out in enumerate(outs):
        place = me[0] * len(outs) + step

        @pl.when(kinds[place] == 1)
        def _():
            out[0] = nesterov(scale, gv[index[place]], mv[index[place]])
            out[1] = nesterov(scale, sib[0, start + step], sib[1, start + step])


def form_near_kernel(devices, me, kinds, index, clip, gv, mv, sib, kg, km, mirror, kv_sib, out):
    scale = clip[0:1, 0:1]
    rows, kv_rows = gv.shape[1], kg.shape[1]
    mine = (me[0] >= devices // 2).astype(jnp.int32)
    for step in range(out.shape[0]):
        place = me[0] * out.shape[0] + step

        @pl.when(kinds[place] == 1)
        def _():
            out[step, 0, :rows] = nesterov(scale, gv[index[place]], mv[index[place]])
            out[step, 1, :rows] = nesterov(scale, sib[0, step], sib[1, step])

        @pl.when(kinds[place] == 2)
        def _():
            for core, low, grad, moment in (
                (0, 0, kg[mine], km[mine]),
                (0, kv_rows, mirror[0], mirror[1]),
                (1, 0, kv_sib[0, 0], kv_sib[0, 1]),
                (1, kv_rows, kv_sib[1, 0], kv_sib[1, 1]),
            ):
                out[step, core, low : low + kv_rows] = nesterov(scale, grad, moment)


def form_call(kernel, name, table, owners, me, operands, outs):
    kinds, index = visits(table, owners)
    vmem = pl.BlockSpec(memory_space=pltpu.VMEM)
    smem = pl.BlockSpec(memory_space=pltpu.SMEM)
    return pl.pallas_call(
        kernel,
        in_specs=[smem] * 3 + [vmem] * len(operands),
        out_specs=[vmem] * len(outs),
        out_shape=outs,
        compiler_params=pltpu.CompilerParams(vmem_limit_bytes=STREAM_LIMIT),
        name=name,
    )(me, kinds, index, *operands)


def form_far(me, table, squares, gv, mv, sib, count):
    devices = table.shape[1]
    steps = devices // 4
    outs = [jax.ShapeDtypeStruct((8, 128), F32)]
    outs += [jax.ShapeDtypeStruct((2,) + gv.shape[1:], BF16)] * steps
    kernel = functools.partial(form_far_kernel, count, steps)
    owners = far_owners(devices, 0)
    return form_call(kernel, "far", table, owners, me, (squares, gv, mv, sib), outs)


def form_near(me, table, clip, gv, mv, sib, kg, km, mirror, kv_sib):
    _, rows, width = gv.shape
    devices = table.shape[1]
    outs = [
        jax.ShapeDtypeStruct((devices // 4, 2, max(rows, 2 * kg.shape[1]), width), BF16)
    ]
    operands = (clip, gv, mv, sib, kg, km, mirror, kv_sib)
    kernel = functools.partial(form_near_kernel, devices)
    return form_call(kernel, "form", table, near_owners(devices, 0), me, operands, outs)[0]


def dot(left, right):
    return jnp.dot(left, right, preferred_element_type=F32)


def apply_rows(gain, x, rest, lead, low, high, store):
    width = x.shape[1]
    chunk = 512 if width % 512 == 0 else width
    for start in range(0, width, chunk):
        part = x[low:high, start : start + chunk].astype(F32)
        value = lead[low:high, 0:1] * part + dot(rest[low:high], x[:, start : start + chunk])
        value = (gain * value.astype(BF16).astype(F32)).astype(BF16)
        store(start, chunk, value)


def outer(left, right):
    return lax.dot_general(left, right, (((1,), (1,)), ((), ())), preferred_element_type=F32)


def diagonal_blocks(size):
    step = 128 if size % 128 == 0 else size
    row = lax.broadcasted_iota(jnp.int32, (step, step), 0)
    col = lax.broadcasted_iota(jnp.int32, (step, step), 1)
    return row == col, [slice(low, low + step) for low in range(0, size, step)]


def transform(gram, rest, lead):
    size = gram.shape[0]
    mask, parts = diagonal_blocks(size)
    trace = sum(
        jnp.sum(jnp.where(mask, gram[part, part], 0.0), keepdims=True) for part in parts
    )
    inverse = 1.0 / (jnp.sqrt(trace) + NORM_EPS)
    scaled = gram[...] * (inverse * inverse)
    low = scaled.astype(BF16)
    first = (NS_B * low.astype(F32) + NS_C * dot(low, low)).astype(BF16)
    product = dot(first, low)
    scaled = (NS_A * NS_A) * scaled + (2.0 * NS_A) * product + dot(product.astype(BF16), first)
    low = scaled.astype(BF16)
    second = (NS_B * low.astype(F32) + NS_C * dot(low, low)).astype(BF16)
    mixed = NS_A * (first.astype(F32) + second.astype(F32)) + dot(second, first)
    gram[...] = mixed * inverse
    for part in parts:
        block = gram[part, part]
        main = jnp.sum(jnp.where(mask, block, 0.0), axis=1, keepdims=True)
        lead[part] = jnp.broadcast_to((NS_A * NS_A) * inverse + main, lead[part].shape)
        gram[part, part] = jnp.where(mask, 0.0, block)
    rest[...] = gram[...].astype(BF16)


def place_blocks(blocks, rows, x, start):
    for index, block in enumerate(blocks):
        for core in range(2):
            low = start + (2 * index + core) * rows
            x[low : low + rows] = block[core, :rows]


def store_blocks(outs, rows):
    def store(start, chunk, value):
        for index, out in enumerate(outs):
            for core in range(2):
                low = (2 * index + core) * rows
                out[core, :rows, start : start + chunk] = value[low : low + rows]

    return store


def split_blocks(ref):
    return [ref.at[index] for index in range(ref.shape[0])]


def near_kernel(rows, me, kinds, near, x, gram):
    @pl.when(kinds[me[0]] == 1)
    def _():
        place_blocks(split_blocks(near), rows, x, 0)
        gram[...] = outer(x[...], x[...])


def transform_kernel(gain, rows, kv_rows, me, kinds, near, near_rows, near_gram, *refs):
    steps = near.shape[0]
    far, (x, rest, lead), outs, gram = (
        refs[:steps], refs[steps : steps + 3], refs[steps + 3 : -1], refs[-1]
    )
    half = near_rows.shape[0]
    kind = kinds[me[0]]

    @pl.when(kind == 1)
    def _():
        x[:half] = near_rows[...]
        place_blocks(far, rows, x, half)
        gram[:half, :half] = near_gram[...]
        cross = outer(near_rows[...], x[half:])
        gram[:half, half:] = cross
        gram[half:, :half] = cross.T
        gram[half:, half:] = outer(x[half:], x[half:])
        transform(gram, rest, lead)
        apply_rows(gain, x, rest, lead, half, 2 * half, store_blocks(outs, rows))

    @pl.when(kind == 2)
    def _():
        size = 4 * kv_rows * steps
        place_blocks(split_blocks(near), 2 * kv_rows, x, 0)
        kv_gram = gram.at[:size, :size]
        kv_gram[...] = outer(x[:size], x[:size])
        transform(kv_gram, rest.at[:size, :size], lead.at[:size])


def apply_kernel(gain, rows, kv_rows, me, kinds, x, rest, lead, out):
    kind = kinds[me[0]]
    blocks = split_blocks(out)

    @pl.when(kind == 1)
    def _():
        apply_rows(gain, x, rest, lead, 0, x.shape[0] // 2, store_blocks(blocks, rows))

    @pl.when(kind == 2)
    def _():
        size = 4 * kv_rows * len(blocks)
        part = x.at[:size], rest.at[:size, :size], lead.at[:size]
        apply_rows(gain, *part, 0, size, store_blocks(blocks, 2 * kv_rows))


def near_product(me, kinds, near, rows):
    width = near.shape[3]
    half = 2 * near.shape[0] * rows
    vmem = pl.BlockSpec(memory_space=pltpu.VMEM)
    smem = pl.BlockSpec(memory_space=pltpu.SMEM)
    return pl.pallas_call(
        functools.partial(near_kernel, rows),
        in_specs=[smem, smem, vmem],
        out_specs=[vmem, vmem],
        out_shape=[
            jax.ShapeDtypeStruct((half, width), BF16),
            jax.ShapeDtypeStruct((half, half), F32),
        ],
        compiler_params=pltpu.CompilerParams(vmem_limit_bytes=STREAM_LIMIT),
        name="near",
    )(me, kinds, near)


def orthogonal_update(me, kinds, near, near_rows, near_gram, far, kv_rows):
    half, width = near_rows.shape
    size = 2 * half
    rows = far[0].shape[1]
    gain = UPDATE_GAIN * math.sqrt(width)
    vmem = pl.BlockSpec(memory_space=pltpu.VMEM)
    smem = pl.BlockSpec(memory_space=pltpu.SMEM)
    params = pltpu.CompilerParams(vmem_limit_bytes=VMEM_LIMIT)
    x, rest, lead, *back = pl.pallas_call(
        functools.partial(transform_kernel, gain, rows, kv_rows),
        in_specs=[smem, smem] + [vmem] * (3 + len(far)),
        out_specs=[vmem] * (3 + len(far)),
        out_shape=[
            jax.ShapeDtypeStruct((size, width), BF16),
            jax.ShapeDtypeStruct((size, size), BF16),
            jax.ShapeDtypeStruct((size, 128), F32),
        ]
        + [jax.ShapeDtypeStruct(block.shape, BF16) for block in far],
        scratch_shapes=[pltpu.VMEM((size, size), F32)],
        compiler_params=params,
        name="transform",
    )(me, kinds, near, near_rows, near_gram, *far)
    near = pl.pallas_call(
        functools.partial(apply_kernel, gain, rows, kv_rows),
        in_specs=[smem, smem] + [vmem] * 3,
        out_specs=vmem,
        out_shape=jax.ShapeDtypeStruct(near.shape, BF16),
        compiler_params=params,
        name="apply",
    )(me, kinds, x, rest, lead)
    return near, back


def gather_near_kernel(rows, kv_rows, me, kinds, near, out, own, theirs):
    for index, block in enumerate(split_blocks(near)):
        out[index] = block[1, :rows]

        @pl.when(kinds[me[0] * near.shape[0] + index] == 2)
        def _():
            for target, core in ((own, 0), (theirs, 1)):
                target[0] = block[core, :kv_rows]
                target[1] = block[core, kv_rows : 2 * kv_rows]


def gather_near(me, table, near, rows, kv_rows):
    steps, _, _, width = near.shape
    kinds, _ = visits(table, near_owners(table.shape[1], 0))
    vmem = pl.BlockSpec(memory_space=pltpu.VMEM)
    smem = pl.BlockSpec(memory_space=pltpu.SMEM)
    return pl.pallas_call(
        functools.partial(gather_near_kernel, rows, kv_rows),
        in_specs=[smem, smem, vmem],
        out_specs=[vmem] * 3,
        out_shape=[jax.ShapeDtypeStruct((steps, rows, width), BF16)]
        + [jax.ShapeDtypeStruct((2, kv_rows, width), BF16)] * 2,
        compiler_params=pltpu.CompilerParams(vmem_limit_bytes=STREAM_LIMIT),
        name="gathernear",
    )(me, kinds, near)


def gather_kernel(*refs):
    for index, block in enumerate(refs[:-1]):
        refs[-1][index] = block[1]


def gather_far(blocks):
    _, rows, width = blocks[0].shape
    vmem = pl.BlockSpec(memory_space=pltpu.VMEM)
    return pl.pallas_call(
        gather_kernel,
        in_specs=[vmem] * len(blocks),
        out_specs=vmem,
        out_shape=jax.ShapeDtypeStruct((len(blocks), rows, width), BF16),
        compiler_params=pltpu.CompilerParams(vmem_limit_bytes=STREAM_LIMIT),
        name="gather",
    )(*blocks)


def kv_kernel(devices, me, near, back, kw, ko, kb, ku):
    mine = (me[0] >= devices // 2).astype(jnp.int32)
    for index, update in ((mine, near[0]), (1 - mine, back[...])):
        value = kw[index] * (1.0 - RATE * DECAY) - RATE * update.astype(F32)
        ko[index] = value
        kb[index] = value.astype(BF16)
        ku[index] = update


def finish_kv(me, devices, near, back, kw):
    vmem = pl.BlockSpec(memory_space=pltpu.VMEM)
    return pl.pallas_call(
        functools.partial(kv_kernel, devices),
        in_specs=[pl.BlockSpec(memory_space=pltpu.SMEM)] + [vmem] * 3,
        out_specs=[vmem] * 3,
        out_shape=[jax.ShapeDtypeStruct(kw.shape, kind) for kind in (F32, BF16, BF16)],
        compiler_params=pltpu.CompilerParams(vmem_limit_bytes=STREAM_LIMIT),
        name="kv",
    )(me, near, back, kw)


def finish_kernel(plan, me, kinds, held, *refs):
    starts, has_earlier, steps, idle = plan
    sources, ew, refs = refs[: len(starts)], refs[len(starts)], refs[len(starts) + 1 :]
    earlier, (new_ref, low_ref, update_ref) = refs[:-3], refs[-3:]
    now = pl.program_id(0)

    if has_earlier and idle:
        first = me[0] * steps
        busy = sum((kinds[first + step] == 1).astype(jnp.int32) for step in range(steps))

        @pl.when(jnp.logical_and(now == 0, busy == 0))
        def _():
            for before, after in zip(earlier, refs[-3:]):
                pltpu.sync_copy(before.at[pl.ds(held[first], 1)], after)

    valid = kinds[me[0] * steps + now] == 1
    for source, (low, high) in zip(sources, starts):
        here = jnp.logical_and(now >= low, now < high)

        @pl.when(jnp.logical_and(here, valid))
        def _():
            update = source[0, 0, : ew.shape[1]]
            value = ew[0] * (1.0 - RATE * DECAY) - RATE * update.astype(F32)
            new_ref[0] = value
            low_ref[0] = value.astype(BF16)
            update_ref[0] = update


def finish(me, table, ew, sources, owners, earlier):
    _, rows, width = ew.shape
    owners = joined(*owners)
    kinds, held = visits(table, owners)
    idle = not (visit_tables(table, owners)[0] == 1).any(axis=1).all()
    size = len(owners[0])
    spec = pl.BlockSpec((1, rows, width), lambda i, me, k, h: (h[me[0] * size + i], 0, 0))
    operands, in_specs, starts = [me, kinds, held], [], []
    low = 0
    for source in sources:
        steps, _, source_rows, _ = source.shape
        in_specs.append(
            pl.BlockSpec(
                (1, 1, source_rows, width),
                lambda i, *_, low=low, steps=steps: (jnp.clip(i - low, 0, steps - 1), 0, 0, 0),
            )
        )
        operands.append(source)
        starts.append((low, low + steps))
        low += steps
    in_specs.append(spec)
    operands.append(ew)
    aliases = {}
    if earlier is not None:
        aliases = {len(operands) + index: index for index in range(3)}
        in_specs += [pl.BlockSpec(memory_space=pl.ANY)] * 3
        operands += list(earlier)
    return pl.pallas_call(
        functools.partial(finish_kernel, (starts, earlier is not None, size, idle)),
        grid_spec=pltpu.PrefetchScalarGridSpec(
            num_scalar_prefetch=3,
            grid=(size,),
            in_specs=in_specs,
            out_specs=[spec] * 3,
        ),
        out_shape=[jax.ShapeDtypeStruct(ew.shape, kind) for kind in (F32, BF16, BF16)],
        input_output_aliases=aliases,
        compiler_params=pltpu.CompilerParams(vmem_limit_bytes=STREAM_LIMIT),
        name="finish",
    )(*operands)


def permute(array, pairs):
    return lax.ppermute(array, "fsdp", pairs)


def together(*arrays):
    return lax.optimization_barrier(arrays)


def far_pairs(table, step, to_owners):
    devices = table.shape[1]
    pairs = [(d ^ (2 * step), d) for d in range(devices) if table[0, d] == 1]
    return pairs if to_owners else [(there, here) for here, there in pairs]


def exchange_near(blocks, devices):
    groups = [near_owners(devices, 0)[first] for first in (0, 1, devices // 2, devices // 2 + 1)]
    return lax.all_to_all(blocks, "fsdp", 0, 0, axis_index_groups=groups, tiled=True)


def shards(expert_grad, expert_momentum, expert_master, kv_grad, kv_momentum, kv_master):
    devices = lax.axis_size("fsdp")
    chips = devices // 2
    far_steps = range(chips // 2, chips)
    me = lax.axis_index("fsdp").reshape(1)
    shape = expert_grad.shape
    rows, width = shape[2], shape[3]
    kv_rows = kv_grad.shape[1]
    flat = lambda array: array.reshape(-1, rows, width)
    eg, em, ew = flat(expert_grad), flat(expert_momentum), flat(expert_master)
    table = owner_table(eg.shape[0], kv_grad.shape[0], devices)
    kinds = jnp.asarray(table[0])
    count = CLIP_RATIO * math.sqrt(devices * (expert_grad.size + kv_grad.size))
    cores = [(device, device ^ 1) for device in range(devices)]
    mirrors = [(device, device ^ chips) for device in range(devices)]
    near_own, near_other = near_owners(devices, 0), near_owners(devices, 1)
    far_own, far_other = far_owners(devices, 0), far_owners(devices, 1)

    partial, gv, mv, kg, km = load(eg, em, kv_grad, kv_momentum, devices)
    squares = lax.all_to_all(partial, "fsdp", 0, 0, tiled=True)
    staged, keep, away = stage(me, table, gv, mv, kg, km)
    mirror, sibling = permute(away, mirrors), permute(staged, cores)
    squares, sibling, mirror = together(squares, sibling, mirror)

    clip, *far = form_far(me, table, squares, gv, mv, sibling, count)
    clip, far[0] = together(clip, far[0])
    kv_sibling = permute(jnp.stack([keep, mirror]), [pair for pair in cores if pair[1] % 2])
    near = form_near(me, table, clip, gv, mv, sibling, kg, km, mirror, kv_sibling)
    far = [permute(block, far_pairs(table, step, True)) for step, block in zip(far_steps, far)]
    near = exchange_near(near, devices)

    near_rows, near_gram = near_product(me, kinds, near, rows)

    near_rows, clip = together(near_rows, clip)
    factor = clip[0, 0]
    expert_moment_out = MOMENTUM * expert_momentum + factor * expert_grad
    kv_moment_out = MOMENTUM * kv_momentum + factor * kv_grad
    near_rows, expert_moment_out, kv_moment_out = together(
        near_rows, expert_moment_out, kv_moment_out
    )
    near, far = orthogonal_update(me, kinds, near, near_rows, near_gram, far, kv_rows)

    far = [permute(block, far_pairs(table, step, False)) for step, block in zip(far_steps, far)]
    near = exchange_near(near, devices)
    near_sibling, kv_own, kv_theirs = gather_near(me, table, near, rows, kv_rows)
    near_sibling = permute(near_sibling, cores)
    kv_theirs = permute(kv_theirs, [pair for pair in cores if pair[0] % 2])
    kv_own = jnp.where(me[0] % 2 == 1, kv_own, kv_theirs)
    kv_back = permute(kv_own[1], mirrors)
    done = finish(me, table, ew, [near], [near_own], None)
    far[0], *done = together(far[0], *done)
    far_sibling = permute(gather_far(far), cores)
    sources = [block[None] for block in far] + [near_sibling[:, None]]
    done = finish(me, table, ew, sources, [far_own, near_other], done)
    kv_back, *done = together(kv_back, *done)
    ko, kb, ku = finish_kv(me, devices, kv_own, kv_back, kv_master)
    eo, eb, eu = finish(me, table, ew, [far_sibling[:, None]], [far_other], done)
    return (
        eo.reshape(shape),
        expert_moment_out,
        eb.reshape(shape),
        eu.reshape(shape),
        ko,
        kv_moment_out,
        kb,
        ku,
    )


def solution(mesh):
    expert = P("groups", None, "fsdp", None)
    kv = P("groups", "fsdp", None)
    return jax.shard_map(
        shards,
        mesh=mesh,
        in_specs=(expert, expert, expert, kv, kv, kv),
        out_specs=(expert, expert, expert, expert, kv, kv, kv, kv),
        check_vma=False,
    )
```

profile of v0, /device:TPU:7, one launch (start us, length us, event | category | flops | bytes accessed | tf_op | source)
XLA Modules:
  0.0 186.1 jit_solution(1970675479681433413)
XLA Ops:
  2.7 3.9 %load.1 = (f32[16,8,128]{2,1,0:T(8,128)S(1)}, f32[12,48,2048]{2,1,0:T(8,128)S(1)}, f32[12,48,2048]{2,1,0:T(8,128)S(1)}, f32[2,32,2048]{2,1,0:T(8,128)S(1)}, f32[2,32,2048]{2,1,0:T(8,128)S(1)}) custom-call(f32[12,48,2048]{2,1,0:T(8,128)} %bitcast.30, f32[12,48,2048]{2,1,0:T(8,128)} %bitcast.31, f32[2,32,2048]{2,1,0:T(8,128)S(1)} %copy-done.3, ...), custom_call_target="tpu_custom_call" | custom-call | tf_op jit(solution)/shard_map/load/pallas_call | solution.py:121
  8.3 2.3 %collective-permute-start.1 = (bf16[2,32,2048]{2,1,0:T(8,128)(2,1)S(1)}, bf16[2,32,2048]{2,1,0:T(8,128)(2,1)S(1)}, u32[]{:S(2)}, u32[]{:S(2)}) collective-permute-start(bf16[2,32,2048]{2,1,0:T(8,128)(2,1)S(1)} %get-tuple-element.69), channel_id=1, source_target_pairs={{0,8},{1,9},{2,10},{3,11},{4,12},{5,13},{6,14},{7,15},{8,0},{9,1},... | collective-permute-start | bytes 786440 | tf_op jit(solution)/shard_map/ppermute | solution.py:552
  10.6 13.7 %all_to_all.15.squares = f32[16,8,128]{2,1,0:T(8,128)S(1)} all-to-all(f32[16,8,128]{2,1,0:T(8,128)S(1)} %get-tuple-element.63), channel_id=1, replica_groups=mesh['groups'=2,'fsdp'=16] {'fsdp'}, dimensions={0} | all-to-all | bytes 131072 | tf_op jit(solution)/shard_map/all_to_all | solution.py:589
  24.4 1.3 collective-permute-start.2
  25.7 2.1 %far.1 = (f32[8,128]{1,0:T(8,128)S(1)}, bf16[2,48,2048]{2,1,0:T(8,128)(2,1)}, bf16[2,48,2048]{2,1,0:T(8,128)(2,1)}, bf16[2,48,2048]{2,1,0:T(8,128)(2,1)S(1)}, bf16[2,48,2048]{2,1,0:T(8,128)(2,1)S(1)}) custom-call(s32[1]{0:T(128)} %bitcast.me, s32[64]{0:T(128)S(1)} %copy-done.18, s32[64]{0:T(128)S(1)} %copy-done.17, f32[16,8,128]{2,1,0:T(8,128)S(1)} %all_to_all.15.squares, ...), custom_call_target="tpu_custom_call" | custom-call | tf_op jit(solution)/shard_map/far/pallas_call | solution.py:212
  28.7 1.6 form.1
  30.2 1.3 copy-done.2
  31.6 4.7 %all-to-all-start.1 = ((bf16[4,2,64,2048]{3,2,1,0:T(8,128)(2,1)}), bf16[4,2,64,2048]{3,2,1,0:T(8,128)(2,1)S(1)}, u32[]{:S(2)}, u32[]{:S(2)}) async-start(bf16[4,2,64,2048]{3,2,1,0:T(8,128)(2,1)} %copy-done.2), calls=%async_computation.1 | async-start | bytes 4194304 | tf_op jit(solution)/shard_map/all_to_all | solution.py:567
  36.3 4.2 %collective-permute-start.3 = (bf16[2,48,2048]{2,1,0:T(8,128)(2,1)}, bf16[2,48,2048]{2,1,0:T(8,128)(2,1)S(1)}, u32[]{:S(2)}, u32[]{:S(2)}) collective-permute-start(bf16[2,48,2048]{2,1,0:T(8,128)(2,1)} %get-tuple-element.82), channel_id=1, source_target_pairs={{8,0},{9,1},{10,2},{12,4},{14,6},{15,7},{0,8},{2,10},{3,11},{4,12}... | collective-permute-start | bytes 1179656 | tf_op jit(solution)/shard_map/ppermute | solution.py:552
  41.8 8.6 %collective-permute-start.6 = (bf16[2,48,2048]{2,1,0:T(8,128)(2,1)}, bf16[2,48,2048]{2,1,0:T(8,128)(2,1)}, u32[]{:S(2)}, u32[]{:S(2)}) collective-permute-start(bf16[2,48,2048]{2,1,0:T(8,128)(2,1)} %copy-done.22), channel_id=1, source_target_pairs={{14,0},{15,1},{12,2},{10,4},{8,6},{9,7},{6,8},{4,10},{5,11},{2,12}... | collective-permute-start | bytes 1179656 | tf_op jit(solution)/shard_map/ppermute | solution.py:552
  50.5 23.2 %all-to-all-done.1.near = bf16[4,2,64,2048]{3,2,1,0:T(8,128)(2,1)S(1)} async-done(((bf16[4,2,64,2048]{3,2,1,0:T(8,128)(2,1)}), bf16[4,2,64,2048]{3,2,1,0:T(8,128)(2,1)S(1)}, u32[]{:S(2)}, u32[]{:S(2)}) %all-to-all-start.1) | async-done | bytes 2097184 | tf_op jit(solution)/shard_map/all_to_all | solution.py:567
  74.8 8.2 %multiply_add_fusion = f32[4,3,48,2048]{3,2,1,0:T(8,128)} fusion(f32[4,3,48,2048]{3,2,1,0:T(8,128)} %param.19, f32[4,3,48,2048]{3,2,1,0:T(8,128)} %param.20, f32[]{:T(128)} %bitcast.5), kind=kLoop, calls=%fused_computation | loop fusion | flops 3538944 | bytes 14155780 | tf_op jit(solution)/shard_map/add | solution.py:605
  83.0 1.5 multiply_add_fusion.1
  84.5 5.6 %transform.1 = (bf16[768,2048]{1,0:T(8,128)(2,1)S(1)}, bf16[768,768]{1,0:T(8,128)(2,1)S(1)}, f32[768,128]{1,0:T(8,128)S(1)}, bf16[2,48,2048]{2,1,0:T(8,128)(2,1)...) custom-call(s32[1]{0:T(128)} %bitcast.me, s32[16]{0:T(128)S(1)} %copy-done.11, ...), custom_call_target="tpu_custom_call" | custom-call | tf_op jit(solution)/shard_map/transform/pallas_call | solution.py:390
  90.1 2.0 %apply.1 = bf16[4,2,64,2048]{3,2,1,0:T(8,128)(2,1)S(1)} custom-call(s32[1]{0:T(128)} %bitcast.me, s32[16]{0:T(128)S(1)} %copy-done.11, bf16[768,2048]{1,0:T(8,128)(2,1)S(1)} %get-tuple-element.87.x, bf16[768,768]{1,0:T(8,128)(2,1)S(1)} %get-tuple-element.88.rest, f32[768,128]{1,0:T(8,128)S(1)} %get-tuple-element.89.lead), custom_call_target="tpu_custom_call" | custom-call | tf_op jit(solution)/shard_map/apply/pallas_call | solution.py:404
  92.1 1.3 copy-done.1
  93.4 10.5 %all-to-all-start.2 = ((bf16[4,2,64,2048]{3,2,1,0:T(8,128)(2,1)}), bf16[4,2,64,2048]{3,2,1,0:T(8,128)(2,1)S(1)}, u32[]{:S(2)}, u32[]{:S(2)}) async-start(bf16[4,2,64,2048]{3,2,1,0:T(8,128)(2,1)} %copy-done.1), calls=%async_computation.2 | async-start | bytes 4194304 | tf_op jit(solution)/shard_map/all_to_all | solution.py:567
  104.0 1.3 collective-permute-start.7
  106.0 1.4 collective-permute-start.9
  107.4 1.3 collective-permute-start.10
  108.7 30.9 %all-to-all-done.2.refs_0_.near = bf16[4,2,64,2048]{3,2,1,0:T(8,128)(2,1)S(1)} async-done(((bf16[4,2,64,2048]{3,2,1,0:T(8,128)(2,1)}), bf16[4,2,64,2048]{3,2,1,0:T(8,128)(2,1)S(1)}, u32[]{:S(2)}, u32[]{:S(2)}) %all-to-all-start.2) | async-done | bytes 2097184 | tf_op jit(solution)/shard_map/all_to_all | solution.py:567
  139.6 1.3 gathernear.1
  142.5 17.8 %collective-permute-start.12 = (bf16[2,32,2048]{2,1,0:T(8,128)(2,1)}, bf16[2,32,2048]{2,1,0:T(8,128)(2,1)}, u32[]{:S(2)}, u32[]{:S(2)}) collective-permute-start(bf16[2,32,2048]{2,1,0:T(8,128)(2,1)} %get-tuple-element.98), channel_id=1, source_target_pairs={{1,0},{3,2},{5,4},{7,6},{9,8},{11,10},{13,12},{15,14},{17,16},{19,... | collective-permute-start | bytes 786440 | tf_op jit(solution)/shard_map/ppermute | solution.py:552
  160.3 2.3 %copy-done = f32[4,3,48,2048]{3,2,1,0:T(8,128)S(1)} copy-done((f32[4,3,48,2048]{3,2,1,0:T(8,128)S(1)}, f32[4,3,48,2048]{3,2,1,0:T(8,128)}, u32[]{:S(2)}) %copy-start) | copy-done | bytes 4718616
  162.7 2.0 %finish.3 = (f32[12,48,2048]{2,1,0:T(8,128)}, bf16[12,48,2048]{2,1,0:T(8,128)(2,1)}, bf16[12,48,2048]{2,1,0:T(8,128)(2,1)}) custom-call(s32[1]{0:T(128)} %bitcast.me, s32[64]{0:T(128)S(1)} %copy-done.10, s32[64]{0:T(128)S(1)} %copy-done.12, bf16[4,2,64,2048]{3,2,1,0:T(8,128)(2,1)S(1)} %all-to-all-done.2.refs_0_.near, f32[12,48,2048]{2,1,0:T(8,128)S(1)} %bitcast.18), custom_call_target="tpu_custom_call" | custom-call | tf_op jit(solution)/shard_map/finish/pallas_call | solution.py:536
  164.8 1.3 gather.1
  166.0 1.5 collective-permute-start.11
  167.6 7.9 %collective-permute-start.13 = (bf16[32,2048]{1,0:T(8,128)(2,1)S(1)}, bf16[32,2048]{1,0:T(8,128)(2,1)S(1)}, u32[]{:S(2)}, u32[]{:S(2)}) collective-permute-start(bf16[32,2048]{1,0:T(8,128)(2,1)S(1)} %slice_bitcast_fusion), channel_id=1, source_target_pairs={{0,8},{1,9},{2,10},{3,11},{4,12},{5,13},{6,14},{7,15},{8,0},{9,1},... | collective-permute-start | bytes 393224 | tf_op jit(solution)/shard_map/ppermute | solution.py:552
  175.6 4.9 %finish.4 = (f32[12,48,2048]{2,1,0:T(8,128)}, bf16[12,48,2048]{2,1,0:T(8,128)(2,1)}, bf16[12,48,2048]{2,1,0:T(8,128)(2,1)}) custom-call(s32[1]{0:T(128)} %bitcast.me, s32[128]{0:T(128)S(1)} %copy-done.16, s32[128]{0:T(128)S(1)} %copy-done.15, bf16[1,2,48,2048]{3,2,1,0:T(8,128)(2,1)S(1)} %bitcast.23, ...), custom_call_target="tpu_custom_call", output_to_operand_aliasing={{0}: (9, {}), {1}: (10, {}), {2}: (11, {})} | custom-call | tf_op jit(solution)/shard_map/finish/pallas_call | solution.py:536
  180.5 1.7 collective-permute-done.13.back
  182.3 1.1 kv.1
  183.3 2.8 %finish.5 = (f32[12,48,2048]{2,1,0:T(8,128)}, bf16[12,48,2048]{2,1,0:T(8,128)(2,1)}, bf16[12,48,2048]{2,1,0:T(8,128)(2,1)}) custom-call(s32[1]{0:T(128)} %bitcast.me, s32[64]{0:T(128)S(1)} %copy-done.14, s32[64]{0:T(128)S(1)} %copy-done.13, bf16[4,1,48,2048]{3,2,1,0:T(8,128)(2,1)S(1)} %bitcast.26, ...), custom_call_target="tpu_custom_call", output_to_operand_aliasing={{0}: (5, {}), {1}: (6, {}), {2}: (7, {})} | custom-call | tf_op jit(solution)/shard_map/finish/pallas_call | solution.py:536
  (75 shorter events, 9.6 us)
Async XLA Ops:
  6.6 19.1 %copy-start.17 = (s32[64]{0:T(128)S(1)}, s32[64]{0:T(128)}, u32[]{:S(2)}) copy-start(s32[64]{0:T(128)} %constant.44.clone.index) | copy-start | bytes 772
  6.6 19.1 %copy-start.18 = (s32[64]{0:T(128)S(1)}, s32[64]{0:T(128)}, u32[]{:S(2)}) copy-start(s32[64]{0:T(128)} %constant.43.clone.kinds) | copy-start | bytes 772
  7.5 16.7 %collective-permute-start = (bf16[2,8,48,2048]{3,2,1,0:T(8,128)(2,1)S(1)}, bf16[2,8,48,2048]{3,2,1,0:T(8,128)(2,1)S(1)}, u32[]{:S(2)}, u32[]{:S(2)}) collective-permute-start(bf16[2,8,48,2048]{3,2,1,0:T(8,128)(2,1)S(1)} %get-tuple-element.68), channel_id=1, source_target_pairs={{0,1},{1,0},{2,3},{3,2},{4,5},{5,4},{6,7},{7,6},{8,9},{9,8},{10,11... | collective-permute-start | bytes 9437192 | tf_op jit(solution)/shard_map/ppermute | solution.py:552
  8.3 16.0 %collective-permute-start.1 = (bf16[2,32,2048]{2,1,0:T(8,128)(2,1)S(1)}, bf16[2,32,2048]{2,1,0:T(8,128)(2,1)S(1)}, u32[]{:S(2)}, u32[]{:S(2)}) collective-permute-start(bf16[2,32,2048]{2,1,0:T(8,128)(2,1)S(1)} %get-tuple-element.69), channel_id=1, source_target_pairs={{0,8},{1,9},{2,10},{3,11},{4,12},{5,13},{6,14},{7,15},{8,0},{9,1},... | collective-permute-start | bytes 786440 | tf_op jit(solution)/shard_map/ppermute | solution.py:552
  24.3 4.3 %copy-start.10 = (s32[64]{0:T(128)S(1)}, s32[64]{0:T(128)}, u32[]{:S(2)}) copy-start(s32[64]{0:T(128)} %constant.45.clone.kinds) | copy-start | bytes 772
  24.4 4.3 %copy-start.12 = (s32[64]{0:T(128)S(1)}, s32[64]{0:T(128)}, u32[]{:S(2)}) copy-start(s32[64]{0:T(128)} %constant.46.clone.index.held) | copy-start | bytes 772
  24.4 4.3 %collective-permute-start.2 = (bf16[2,2,32,2048]{3,2,1,0:T(8,128)(2,1)S(1)}, bf16[2,2,32,2048]{3,2,1,0:T(8,128)(2,1)S(1)}, u32[]{:S(2)}, u32[]{:S(2)}) collective-permute-start(bf16[2,2,32,2048]{3,2,1,0:T(8,128)(2,1)S(1)} %pad_maximum_fusion), channel_id=1, source_target_pairs={{0,1},{2,3},{4,5},{6,7},{8,9},{10,11},{12,13},{14,15},{16,17},{18,... | collective-permute-start | bytes 1572872 | tf_op jit(solution)/shard_map/ppermute | solution.py:552
  28.7 45.0 %copy-start.11 = (s32[16]{0:T(128)S(1)}, s32[16]{0:T(128)}, u32[]{:S(2)}) copy-start(s32[16]{0:T(128)} %constant.41.clone.kinds) | copy-start | bytes 196
  31.6 42.1 %all-to-all-start.1 = ((bf16[4,2,64,2048]{3,2,1,0:T(8,128)(2,1)}), bf16[4,2,64,2048]{3,2,1,0:T(8,128)(2,1)S(1)}, u32[]{:S(2)}, u32[]{:S(2)}) async-start(bf16[4,2,64,2048]{3,2,1,0:T(8,128)(2,1)} %copy-done.2), calls=%async_computation.1 | async-start | bytes 4194304 | tf_op jit(solution)/shard_map/all_to_all | solution.py:567
  36.3 48.2 %collective-permute-start.3 = (bf16[2,48,2048]{2,1,0:T(8,128)(2,1)}, bf16[2,48,2048]{2,1,0:T(8,128)(2,1)S(1)}, u32[]{:S(2)}, u32[]{:S(2)}) collective-permute-start(bf16[2,48,2048]{2,1,0:T(8,128)(2,1)} %get-tuple-element.82), channel_id=1, source_target_pairs={{8,0},{9,1},{10,2},{12,4},{14,6},{15,7},{0,8},{2,10},{3,11},{4,12}... | collective-permute-start | bytes 1179656 | tf_op jit(solution)/shard_map/ppermute | solution.py:552
  40.5 44.0 %collective-permute-start.4 = (bf16[2,48,2048]{2,1,0:T(8,128)(2,1)}, bf16[2,48,2048]{2,1,0:T(8,128)(2,1)S(1)}, u32[]{:S(2)}, u32[]{:S(2)}) collective-permute-start(bf16[2,48,2048]{2,1,0:T(8,128)(2,1)} %get-tuple-element.83), channel_id=1, source_target_pairs={{10,0},{11,1},{8,2},{14,4},{12,6},{13,7},{2,8},{0,10},{1,11},{6,12... | collective-permute-start | bytes 1179656 | tf_op jit(solution)/shard_map/ppermute | solution.py:552
  41.2 43.3 %collective-permute-start.5 = (bf16[2,48,2048]{2,1,0:T(8,128)(2,1)}, bf16[2,48,2048]{2,1,0:T(8,128)(2,1)S(1)}, u32[]{:S(2)}, u32[]{:S(2)}) collective-permute-start(bf16[2,48,2048]{2,1,0:T(8,128)(2,1)} %copy-done.23), channel_id=1, source_target_pairs={{12,0},{13,1},{14,2},{8,4},{10,6},{11,7},{4,8},{6,10},{7,11},{0,12... | collective-permute-start | bytes 1179656 | tf_op jit(solution)/shard_map/ppermute | solution.py:552
  41.8 42.6 %collective-permute-start.6 = (bf16[2,48,2048]{2,1,0:T(8,128)(2,1)}, bf16[2,48,2048]{2,1,0:T(8,128)(2,1)}, u32[]{:S(2)}, u32[]{:S(2)}) collective-permute-start(bf16[2,48,2048]{2,1,0:T(8,128)(2,1)} %copy-done.22), channel_id=1, source_target_pairs={{14,0},{15,1},{12,2},{10,4},{8,6},{9,7},{6,8},{4,10},{5,11},{2,12}... | collective-permute-start | bytes 1179656 | tf_op jit(solution)/shard_map/ppermute | solution.py:552
  74.8 8.2 %copy-start.4 = (f32[2,32,2048]{2,1,0:T(8,128)S(1)}, f32[2,32,2048]{2,1,0:T(8,128)}, u32[]{:S(2)}) copy-start(f32[2,32,2048]{2,1,0:T(8,128)} %kg.1) | copy-start | bytes 1572868
  74.8 8.2 %copy-start.6 = (f32[2,32,2048]{2,1,0:T(8,128)S(1)}, f32[2,32,2048]{2,1,0:T(8,128)}, u32[]{:S(2)}) copy-start(f32[2,32,2048]{2,1,0:T(8,128)} %km.1) | copy-start | bytes 1572868
  93.4 46.1 %all-to-all-start.2 = ((bf16[4,2,64,2048]{3,2,1,0:T(8,128)(2,1)}), bf16[4,2,64,2048]{3,2,1,0:T(8,128)(2,1)S(1)}, u32[]{:S(2)}, u32[]{:S(2)}) async-start(bf16[4,2,64,2048]{3,2,1,0:T(8,128)(2,1)} %copy-done.1), calls=%async_computation.2 | async-start | bytes 4194304 | tf_op jit(solution)/shard_map/all_to_all | solution.py:567
  104.0 60.7 %collective-permute-start.7 = (bf16[2,48,2048]{2,1,0:T(8,128)(2,1)}, bf16[2,48,2048]{2,1,0:T(8,128)(2,1)S(1)}, u32[]{:S(2)}, u32[]{:S(2)}) collective-permute-start(bf16[2,48,2048]{2,1,0:T(8,128)(2,1)} %get-tuple-element.86), channel_id=1, source_target_pairs={{0,8},{1,9},{2,10},{4,12},{6,14},{7,15},{8,0},{10,2},{11,3},{12,4}... | collective-permute-start | bytes 1179656 | tf_op jit(solution)/shard_map/ppermute | solution.py:552
  105.3 59.5 %collective-permute-start.8 = (bf16[2,48,2048]{2,1,0:T(8,128)(2,1)}, bf16[2,48,2048]{2,1,0:T(8,128)(2,1)S(1)}, u32[]{:S(2)}, u32[]{:S(2)}) collective-permute-start(bf16[2,48,2048]{2,1,0:T(8,128)(2,1)} %get-tuple-element.94), channel_id=1, source_target_pairs={{0,10},{1,11},{2,8},{4,14},{6,12},{7,13},{8,2},{10,0},{11,1},{12,6... | collective-permute-start | bytes 1179656 | tf_op jit(solution)/shard_map/ppermute | solution.py:552
  106.0 58.8 %collective-permute-start.9 = (bf16[2,48,2048]{2,1,0:T(8,128)(2,1)}, bf16[2,48,2048]{2,1,0:T(8,128)(2,1)}, u32[]{:S(2)}, u32[]{:S(2)}) collective-permute-start(bf16[2,48,2048]{2,1,0:T(8,128)(2,1)} %get-tuple-element.95), channel_id=1, source_target_pairs={{0,12},{1,13},{2,14},{4,8},{6,10},{7,11},{8,4},{10,6},{11,7},{12,0... | collective-permute-start | bytes 1179656 | tf_op jit(solution)/shard_map/ppermute | solution.py:552
  107.4 57.4 %collective-permute-start.10 = (bf16[2,48,2048]{2,1,0:T(8,128)(2,1)}, bf16[2,48,2048]{2,1,0:T(8,128)(2,1)}, u32[]{:S(2)}, u32[]{:S(2)}) collective-permute-start(bf16[2,48,2048]{2,1,0:T(8,128)(2,1)} %get-tuple-element.96), channel_id=1, source_target_pairs={{0,14},{1,15},{2,12},{4,10},{6,8},{7,9},{8,6},{10,4},{11,5},{12,2}... | collective-permute-start | bytes 1179656 | tf_op jit(solution)/shard_map/ppermute | solution.py:552
  139.6 36.0 %slice-start = ((s8[4718592]{0:T(1024)(128)(4,1)}), s8[524288]{0:T(1024)(128)(4,1)S(1)}, s32[]{:S(2)}) async-start(s8[4718592]{0:T(1024)(128)(4,1)} %bitcast.19), calls=%async_computation.3 | async-start | bytes 1048576
  142.5 25.0 %collective-permute-start.12 = (bf16[2,32,2048]{2,1,0:T(8,128)(2,1)}, bf16[2,32,2048]{2,1,0:T(8,128)(2,1)}, u32[]{:S(2)}, u32[]{:S(2)}) collective-permute-start(bf16[2,32,2048]{2,1,0:T(8,128)(2,1)} %get-tuple-element.98), channel_id=1, source_target_pairs={{1,0},{3,2},{5,4},{7,6},{9,8},{11,10},{13,12},{15,14},{17,16},{19,... | collective-permute-start | bytes 786440 | tf_op jit(solution)/shard_map/ppermute | solution.py:552
  162.7 4.9 %copy-start.9 = (bf16[2,32,2048]{2,1,0:T(8,128)(2,1)S(1)}, bf16[2,32,2048]{2,1,0:T(8,128)(2,1)}, u32[]{:S(2)}) copy-start(bf16[2,32,2048]{2,1,0:T(8,128)(2,1)} %copy-done.8) | copy-start | bytes 786436
  162.7 12.9 %slice-start.1 = ((s8[4718592]{0:T(1024)(128)(4,1)}), s8[4194304]{0:T(1024)(128)(4,1)S(1)}, s32[]{:S(2)}) async-start(s8[4718592]{0:T(1024)(128)(4,1)} %bitcast.19), calls=%async_computation.4 | async-start | bytes 8388608
  162.7 12.9 %copy-start.15 = (s32[128]{0:T(128)S(1)}, s32[128]{0:T(128)}, u32[]{:S(2)}) copy-start(s32[128]{0:T(128)} %constant.48.clone.held) | copy-start | bytes 1540
  162.7 12.9 %copy-start.16 = (s32[128]{0:T(128)S(1)}, s32[128]{0:T(128)}, u32[]{:S(2)}) copy-start(s32[128]{0:T(128)} %constant.47.clone.kinds) | copy-start | bytes 1540
  164.7 10.9 %collective-permute-start.14 = (bf16[4,48,2048]{2,1,0:T(8,128)(2,1)S(1)}, bf16[4,48,2048]{2,1,0:T(8,128)(2,1)S(1)}, u32[]{:S(2)}, u32[]{:S(2)}) collective-permute-start(bf16[4,48,2048]{2,1,0:T(8,128)(2,1)S(1)} %copy-done.21), channel_id=1, source_target_pairs={{0,1},{1,0},{2,3},{3,2},{4,5},{5,4},{6,7},{7,6},{8,9},{9,8},{10,11... | collective-permute-start | bytes 2359304 | tf_op jit(solution)/shard_map/ppermute | solution.py:552
  166.0 17.3 %collective-permute-start.11 = (bf16[4,48,2048]{2,1,0:T(8,128)(2,1)S(1)}, bf16[4,48,2048]{2,1,0:T(8,128)(2,1)S(1)}, u32[]{:S(2)}, u32[]{:S(2)}) collective-permute-start(bf16[4,48,2048]{2,1,0:T(8,128)(2,1)S(1)} %gather.1), channel_id=1, source_target_pairs={{0,1},{1,0},{2,3},{3,2},{4,5},{5,4},{6,7},{7,6},{8,9},{9,8},{10,11... | collective-permute-start | bytes 2359304 | tf_op jit(solution)/shard_map/ppermute | solution.py:552
  167.6 14.6 %collective-permute-start.13 = (bf16[32,2048]{1,0:T(8,128)(2,1)S(1)}, bf16[32,2048]{1,0:T(8,128)(2,1)S(1)}, u32[]{:S(2)}, u32[]{:S(2)}) collective-permute-start(bf16[32,2048]{1,0:T(8,128)(2,1)S(1)} %slice_bitcast_fusion), channel_id=1, source_target_pairs={{0,8},{1,9},{2,10},{3,11},{4,12},{5,13},{6,14},{7,15},{8,0},{9,1},... | collective-permute-start | bytes 393224 | tf_op jit(solution)/shard_map/ppermute | solution.py:552
  175.6 6.7 %copy-start.7 = (f32[2,32,2048]{2,1,0:T(8,128)S(1)}, f32[2,32,2048]{2,1,0:T(8,128)}, u32[]{:S(2)}) copy-start(f32[2,32,2048]{2,1,0:T(8,128)} %kw.1) | copy-start | bytes 1572868
  175.6 7.7 %copy-start.13 = (s32[64]{0:T(128)S(1)}, s32[64]{0:T(128)}, u32[]{:S(2)}) copy-start(s32[64]{0:T(128)} %constant.50.clone.held) | copy-start | bytes 772
  175.6 7.7 %copy-start.14 = (s32[64]{0:T(128)S(1)}, s32[64]{0:T(128)}, u32[]{:S(2)}) copy-start(s32[64]{0:T(128)} %constant.49.clone.kinds) | copy-start | bytes 772
  (11 other events, 16.2 us)
where the time goes:
time: 187 us; the launch traced here: 186 us
  starting transfers between devices  65.8 us (35%)
  waiting for transfers between devices  55.9 us (30%)
  Pallas kernels  29.9 us (16%)
  blocking collectives  13.7 us (7%)
  local copies, waits for them, and re-layouts  10.1 us (5%)
  other arithmetic  9.79 us (5%)
    all_to_all x2, waiting for transfers between devices, exchange_near(): lax.all_to_all(blocks, 'fsdp', 0, 0, axis_index_groups=groups, tiled=True)  54.1 us
    ppermute x15, starting transfers between devices, permute(): return lax.ppermute(array, 'fsdp', pairs)  50.6 us
    all_to_all x2, starting transfers between devices, exchange_near(): lax.all_to_all(blocks, 'fsdp', 0, 0, axis_index_groups=groups, tiled=True)  15.2 us
    all_to_all x1, blocking collectives, shards(): squares = lax.all_to_all(partial, 'fsdp', 0, 0, tiled=True)  13.7 us
    pallas_call x3, Pallas kernels, finish(): pl.pallas_call(functools.partial(finish_kernel, (starts, earlier is not N...  9.65 us
    unnamed x52, local copies, waits for them, and re-layouts  9.6 us
    add x1, other arithmetic, shards(): expert_moment_out = MOMENTUM * expert_momentum + factor * expert_grad  8.19 us
    pallas_call x1, Pallas kernels, orthogonal_update(): pl.pallas_call(functools.partial(transform_kernel, gain, rows, kv_rows),...  5.6 us
  transfers between devices with their start and end apart: 17, of which 3 were waited for; matrix products, arithmetic and copies ran while one was open for 6% of the time, Pallas kernels for 7%

commit v1 on v0

v1 whole, which is shorter than its diff:
```python
import functools
import math

import jax
import jax.numpy as jnp
import numpy as np
from jax import lax
from jax.experimental import pallas as pl
from jax.experimental.pallas import tpu as pltpu
from jax.sharding import PartitionSpec as P

NS_A = 3.4445
NS_B = -4.775
NS_C = 2.0315
MOMENTUM = 0.95
RATE = 0.02
DECAY = 0.1
NORM_EPS = 1e-07
CLIP_EPS = 1e-06
CLIP_RATIO = 0.5
UPDATE_GAIN = 0.2

F32 = jnp.float32
BF16 = jnp.bfloat16
VMEM_LIMIT = 40 * 1024 * 1024
LOAD_LIMIT = 42 * 1024 * 1024
STREAM_LIMIT = 16 * 1024 * 1024


def owner_table(experts, kvs, devices):
    table = np.zeros((2, devices), np.int32)
    chips = devices // 2
    first = min(experts, chips)
    for index in range(first):
        table[:, 2 * (index * chips // first)] = (1, index)
    by_parity = sorted(range(chips), key=lambda chip: bin(chip % (chips // 2)).count("1") % 2)
    for index in range(first, experts):
        table[:, 2 * by_parity[index - first] + 1] = (1, index)
    slot = kv_slot(table)
    for index in range(kvs):
        table[:, index * chips + slot] = (2, index)
    return table


def kv_slot(table):
    chips = table.shape[1] // 2
    free = (table[0, :chips] != 1) & (table[0, chips:] != 1)
    return next(slot for slot in range(1, chips, 2) if free[slot])


def near_owners(devices):
    half = devices // 2
    return [[device // half * half + other for other in range(half)] for device in range(devices)]


def far_owners(devices, flip):
    steps = range(devices // 4, devices // 2)
    return [[device ^ (2 * step) ^ flip for step in steps] for device in range(devices)]


class Plan:
    def __init__(self, table):
        self.table = table
        self.parts = []

    def section(self, owners):
        place = sum(part.size for part in self.parts)
        part = np.zeros((len(owners), 2, len(owners[0])), np.int32)
        for device, row in enumerate(owners):
            experts = [self.table[1, owner] for owner in row if self.table[0, owner] == 1]
            last = experts[0] if experts else 0
            for step, owner in enumerate(row):
                last = self.table[1, owner] if self.table[0, owner] == 1 else last
                part[device, :, step] = self.table[0, owner], last
        self.parts.append(part)
        idle = not (part[:, 0] == 1).any(axis=1).all()
        return place, part.shape[2], idle

    def array(self):
        return jnp.asarray(np.concatenate([part.reshape(-1) for part in self.parts]))


def kind_at(section, me, plan, step):
    return plan[section[0] + me[0] * 2 * section[1] + step]


def expert_at(section, me, plan, step):
    return plan[section[0] + (me[0] * 2 + 1) * section[1] + step]


def fold(block, rows):
    parts = block.reshape(-1, rows, block.shape[-1])
    return jnp.sum(parts * parts, axis=0)


def load_kernel(eg, em, total, gv, mv, sems):
    chunks = sems.shape[1]
    size = gv.shape[0] // chunks
    copies = [
        [
            pltpu.make_async_copy(
                source.at[pl.ds(chunk * size, size)],
                target.at[pl.ds(chunk * size, size)],
                sems.at[place, chunk],
            )
            for chunk in range(chunks)
        ]
        for place, (source, target) in enumerate(((eg, gv), (em, mv)))
    ]
    for copy in copies[0] + copies[1]:
        copy.start()
    total[...] = jnp.zeros_like(total)
    for chunk in range(chunks):
        copies[0][chunk].wait()
        total[...] += fold(gv[chunk * size : (chunk + 1) * size], total.shape[0])
    for copy in copies[1]:
        copy.wait()


def load(eg, em):
    vmem = pl.BlockSpec(memory_space=pltpu.VMEM)
    hbm = pl.BlockSpec(memory_space=pltpu.HBM)
    chunks = eg.shape[0] // 3
    total = jax.ShapeDtypeStruct((math.gcd(8, 3 * eg.shape[1]), eg.shape[2]), F32)
    return pl.pallas_call(
        load_kernel,
        in_specs=[hbm] * 2,
        out_specs=[vmem] * 3,
        out_shape=[total] + [jax.ShapeDtypeStruct(eg.shape, F32)] * 2,
        scratch_shapes=[pltpu.SemaphoreType.DMA((2, chunks))],
        compiler_params=pltpu.CompilerParams(vmem_limit_bytes=LOAD_LIMIT),
        name="load",
    )(eg, em)


def stage_kernel(section, devices, me, plan, total, gv, mv, kg, km, partial, staged, away):
    squares = jnp.sum(total[...]) + jnp.sum(fold(kg[...], math.gcd(8, kg.shape[1])))
    partial[...] = jnp.full(partial.shape, squares, F32)
    other = (me[0] < devices // 2).astype(jnp.int32)
    away[0] = kg[other].astype(BF16)
    away[1] = km[other].astype(BF16)
    for step in range(staged.shape[1]):
        expert = expert_at(section, me, plan, step)
        staged[0, step] = gv[expert].astype(BF16)
        staged[1, step] = mv[expert].astype(BF16)


def stage(section, devices, me, plan, total, gv, mv, kg, km):
    _, rows, width = gv.shape
    vmem = pl.BlockSpec(memory_space=pltpu.VMEM)
    smem = pl.BlockSpec(memory_space=pltpu.SMEM)
    return pl.pallas_call(
        functools.partial(stage_kernel, section, devices),
        in_specs=[smem] * 2 + [vmem] * 5,
        out_specs=[vmem] * 3,
        out_shape=[
            jax.ShapeDtypeStruct((devices, 8, 128), F32),
            jax.ShapeDtypeStruct((2, section[1], rows, width), BF16),
            jax.ShapeDtypeStruct((2,) + kg.shape[1:], BF16),
        ],
        compiler_params=pltpu.CompilerParams(vmem_limit_bytes=STREAM_LIMIT),
        name="stage",
    )(me, plan, total, gv, mv, kg, km)


def nesterov(scale, grad, moment):
    clipped = scale * grad.astype(F32)
    return (clipped + MOMENTUM * (MOMENTUM * moment.astype(F32) + clipped)).astype(BF16)


def form_far_kernel(section, count, me, plan, squares, gv, mv, sib, clip, *outs):
    total = jnp.sum(squares[...], axis=0)
    factor = jnp.minimum(1.0, count / (jnp.sqrt(total) + CLIP_EPS))
    clip[...] = factor
    scale = factor[0:1, 0:1]
    for step, out in enumerate(outs):

        @pl.when(kind_at(section, me, plan, step) == 1)
        def _():
            expert = expert_at(section, me, plan, step)
            out[0] = nesterov(scale, gv[expert], mv[expert])
            out[1] = nesterov(scale, sib[0, step], sib[1, step])


def form_far(section, me, plan, squares, gv, mv, sib, count):
    vmem = pl.BlockSpec(memory_space=pltpu.VMEM)
    smem = pl.BlockSpec(memory_space=pltpu.SMEM)
    return pl.pallas_call(
        functools.partial(form_far_kernel, section, count),
        in_specs=[smem] * 2 + [vmem] * 4,
        out_specs=[vmem] * (1 + section[1]),
        out_shape=[jax.ShapeDtypeStruct((8, 128), F32)]
        + [jax.ShapeDtypeStruct((2,) + gv.shape[1:], BF16)] * section[1],
        compiler_params=pltpu.CompilerParams(vmem_limit_bytes=STREAM_LIMIT),
        name="far",
    )(me, plan, squares, gv, mv, sib)


def form_near_kernel(section, me, plan, clip, gv, mv, kg, km, mirror, out):
    scale = clip[0:1, 0:1]
    rows, kv_rows = gv.shape[1], kg.shape[1]
    mine = (me[0] >= section[1]).astype(jnp.int32)
    for step in range(section[1]):
        kind = kind_at(section, me, plan, step)

        @pl.when(kind == 1)
        def _():
            expert = expert_at(section, me, plan, step)
            out[step, :rows] = nesterov(scale, gv[expert], mv[expert])

        @pl.when(kind == 2)
        def _():
            out[step, :kv_rows] = nesterov(scale, kg[mine], km[mine])
            out[step, kv_rows : 2 * kv_rows] = nesterov(scale, mirror[0], mirror[1])


def form_near(section, me, plan, clip, gv, mv, kg, km, mirror):
    _, rows, width = gv.shape
    vmem = pl.BlockSpec(memory_space=pltpu.VMEM)
    smem = pl.BlockSpec(memory_space=pltpu.SMEM)
    return pl.pallas_call(
        functools.partial(form_near_kernel, section),
        in_specs=[smem] * 2 + [vmem] * 6,
        out_specs=vmem,
        out_shape=jax.ShapeDtypeStruct(
            (section[1], max(rows, 2 * kg.shape[1]), width), BF16
        ),
        compiler_params=pltpu.CompilerParams(vmem_limit_bytes=STREAM_LIMIT),
        name="form",
    )(me, plan, clip, gv, mv, kg, km, mirror)


def dot(left, right):
    return jnp.dot(left, right, preferred_element_type=F32)


def apply_rows(gain, x, rest, lead, low, high, store):
    width = x.shape[1]
    chunk = 512 if width % 512 == 0 else width
    for start in range(0, width, chunk):
        part = x[low:high, start : start + chunk].astype(F32)
        value = lead[low:high, 0:1] * part + dot(rest[low:high], x[:, start : start + chunk])
        value = (gain * value.astype(BF16).astype(F32)).astype(BF16)
        store(start, chunk, value)


def outer(left, right):
    return lax.dot_general(left, right, (((1,), (1,)), ((), ())), preferred_element_type=F32)


def diagonal_blocks(size):
    step = 128 if size % 128 == 0 else size
    row = lax.broadcasted_iota(jnp.int32, (step, step), 0)
    col = lax.broadcasted_iota(jnp.int32, (step, step), 1)
    return row == col, [slice(low, low + step) for low in range(0, size, step)]


def transform(gram, rest, lead):
    size = gram.shape[0]
    mask, parts = diagonal_blocks(size)
    trace = sum(
        jnp.sum(jnp.where(mask, gram[part, part], 0.0), keepdims=True) for part in parts
    )
    inverse = 1.0 / (jnp.sqrt(trace) + NORM_EPS)
    scaled = gram[...] * (inverse * inverse)
    low = scaled.astype(BF16)
    first = (NS_B * low.astype(F32) + NS_C * dot(low, low)).astype(BF16)
    product = dot(first, low)
    scaled = (NS_A * NS_A) * scaled + (2.0 * NS_A) * product + dot(product.astype(BF16), first)
    low = scaled.astype(BF16)
    second = (NS_B * low.astype(F32) + NS_C * dot(low, low)).astype(BF16)
    mixed = NS_A * (first.astype(F32) + second.astype(F32)) + dot(second, first)
    gram[...] = mixed * inverse
    for part in parts:
        block = gram[part, part]
        main = jnp.sum(jnp.where(mask, block, 0.0), axis=1, keepdims=True)
        lead[part] = jnp.broadcast_to((NS_A * NS_A) * inverse + main, lead[part].shape)
        gram[part, part] = jnp.where(mask, 0.0, block)
    rest[...] = gram[...].astype(BF16)


def place_far(blocks, x, start):
    rows = blocks[0].shape[1]
    for index, block in enumerate(blocks):
        for core in range(2):
            low = start + (2 * index + core) * rows
            x[low : low + rows] = block[core]


def place_near(blocks, rows, x):
    for index in range(blocks.shape[0]):
        x[index * rows : (index + 1) * rows] = blocks[index, :rows]


def store_far(outs):
    rows = outs[0].shape[1]

    def store(start, chunk, value):
        for index, out in enumerate(outs):
            for core in range(2):
                low = (2 * index + core) * rows
                out[core, :, start : start + chunk] = value[low : low + rows]

    return store


def store_near(out, rows):
    def store(start, chunk, value):
        for index in range(out.shape[0]):
            part = value[index * rows : (index + 1) * rows]
            out[index, :rows, start : start + chunk] = part

    return store


def near_kernel(owns, rows, me, plan, near, x, gram):
    @pl.when(kind_at(owns, me, plan, 0) == 1)
    def _():
        place_near(near, rows, x)
        gram[...] = outer(x[...], x[...])


def transform_kernel(owns, gain, kv_rows, me, plan, near, near_rows, near_gram, *refs):
    steps = (len(refs) - 4) // 2
    far, (x, rest, lead) = refs[:steps], refs[steps : steps + 3]
    outs, gram = refs[steps + 3 : -1], refs[-1]
    half = near_rows.shape[0]
    kind = kind_at(owns, me, plan, 0)

    @pl.when(kind == 1)
    def _():
        x[:half] = near_rows[...]
        place_far(far, x, half)
        gram[:half, :half] = near_gram[...]
        cross = outer(near_rows[...], x[half:])
        gram[:half, half:] = cross
        gram[half:, :half] = cross.T
        gram[half:, half:] = outer(x[half:], x[half:])
        transform(gram, rest, lead)
        apply_rows(gain, x, rest, lead, half, 2 * half, store_far(outs))

    @pl.when(kind == 2)
    def _():
        size = 2 * kv_rows * near.shape[0]
        place_near(near, 2 * kv_rows, x)
        kv_gram = gram.at[:size, :size]
        kv_gram[...] = outer(x[:size], x[:size])
        transform(kv_gram, rest.at[:size, :size], lead.at[:size])


def apply_kernel(owns, gain, rows, kv_rows, me, plan, x, rest, lead, out):
    kind = kind_at(owns, me, plan, 0)

    @pl.when(kind == 1)
    def _():
        apply_rows(gain, x, rest, lead, 0, x.shape[0] // 2, store_near(out, rows))

    @pl.when(kind == 2)
    def _():
        size = 2 * kv_rows * out.shape[0]
        part = x.at[:size], rest.at[:size, :size], lead.at[:size]
        apply_rows(gain, *part, 0, size, store_near(out, 2 * kv_rows))


def near_product(owns, me, plan, near, rows):
    half, width = near.shape[0] * rows, near.shape[2]
    vmem = pl.BlockSpec(memory_space=pltpu.VMEM)
    smem = pl.BlockSpec(memory_space=pltpu.SMEM)
    return pl.pallas_call(
        functools.partial(near_kernel, owns, rows),
        in_specs=[smem, smem, vmem],
        out_specs=[vmem, vmem],
        out_shape=[
            jax.ShapeDtypeStruct((half, width), BF16),
            jax.ShapeDtypeStruct((half, half), F32),
        ],
        compiler_params=pltpu.CompilerParams(vmem_limit_bytes=STREAM_LIMIT),
        name="near",
    )(me, plan, near)


def orthogonal_update(owns, me, plan, near, near_rows, near_gram, far, kv_rows):
    half, width = near_rows.shape
    size = 2 * half
    rows = far[0].shape[1]
    gain = UPDATE_GAIN * math.sqrt(width)
    vmem = pl.BlockSpec(memory_space=pltpu.VMEM)
    smem = pl.BlockSpec(memory_space=pltpu.SMEM)
    params = pltpu.CompilerParams(vmem_limit_bytes=VMEM_LIMIT)
    x, rest, lead, *back = pl.pallas_call(
        functools.partial(transform_kernel, owns, gain, kv_rows),
        in_specs=[smem, smem] + [vmem] * (3 + len(far)),
        out_specs=[vmem] * (3 + len(far)),
        out_shape=[
            jax.ShapeDtypeStruct((size, width), BF16),
            jax.ShapeDtypeStruct((size, size), BF16),
            jax.ShapeDtypeStruct((size, 128), F32),
        ]
        + [jax.ShapeDtypeStruct(block.shape, BF16) for block in far],
        scratch_shapes=[pltpu.VMEM((size, size), F32)],
        compiler_params=params,
        name="transform",
    )(me, plan, near, near_rows, near_gram, *far)
    near = pl.pallas_call(
        functools.partial(apply_kernel, owns, gain, rows, kv_rows),
        in_specs=[smem, smem] + [vmem] * 3,
        out_specs=vmem,
        out_shape=jax.ShapeDtypeStruct(near.shape, BF16),
        compiler_params=params,
        name="apply",
    )(me, plan, x, rest, lead)
    return near, back


def gather_kernel(*refs):
    for index, block in enumerate(refs[:-1]):
        refs[-1][index] = block[1]


def gather_far(blocks):
    _, rows, width = blocks[0].shape
    vmem = pl.BlockSpec(memory_space=pltpu.VMEM)
    return pl.pallas_call(
        gather_kernel,
        in_specs=[vmem] * len(blocks),
        out_specs=vmem,
        out_shape=jax.ShapeDtypeStruct((len(blocks), rows, width), BF16),
        compiler_params=pltpu.CompilerParams(vmem_limit_bytes=STREAM_LIMIT),
        name="gather",
    )(*blocks)


def kv_kernel(devices, me, kv, back, kw, ko, kb, ku):
    mine = (me[0] >= devices // 2).astype(jnp.int32)
    for index, update in ((mine, kv[0, : kw.shape[1]]), (1 - mine, back[...])):
        value = kw[index] * (1.0 - RATE * DECAY) - RATE * update.astype(F32)
        ko[index] = value
        kb[index] = value.astype(BF16)
        ku[index] = update


def finish_kv(me, devices, near, slot, back, kw):
    whole = lambda array: pl.BlockSpec(array.shape, lambda i: (0,) * array.ndim)
    return pl.pallas_call(
        functools.partial(kv_kernel, devices),
        grid=(1,),
        in_specs=[
            pl.BlockSpec(memory_space=pltpu.SMEM),
            pl.BlockSpec((1,) + near.shape[1:], lambda i: (slot, 0, 0)),
            whole(back),
            whole(kw),
        ],
        out_specs=[whole(kw)] * 3,
        out_shape=[jax.ShapeDtypeStruct(kw.shape, kind) for kind in (F32, BF16, BF16)],
        compiler_params=pltpu.CompilerParams(vmem_limit_bytes=STREAM_LIMIT),
        name="kv",
    )(me, near, back, kw)


def finish_kernel(section, starts, me, plan, *refs):
    _, steps, idle = section
    sources, ew, refs = refs[: len(starts)], refs[len(starts)], refs[len(starts) + 1 :]
    earlier, (new_ref, low_ref, update_ref) = refs[:-3], refs[-3:]
    now = pl.program_id(0)

    if earlier and idle:
        kinds = [kind_at(section, me, plan, step) for step in range(steps)]
        busy = sum((kind == 1).astype(jnp.int32) for kind in kinds)

        @pl.when(jnp.logical_and(now == 0, busy == 0))
        def _():
            block = pl.ds(expert_at(section, me, plan, 0), 1)
            for before, after in zip(earlier, refs[-3:]):
                pltpu.sync_copy(before.at[block], after)

    valid = kind_at(section, me, plan, now) == 1
    for source, (low, high) in zip(sources, starts):
        here = jnp.logical_and(now >= low, now < high)

        @pl.when(jnp.logical_and(here, valid))
        def _():
            update = source[0, 0, : ew.shape[1]]
            value = ew[0] * (1.0 - RATE * DECAY) - RATE * update.astype(F32)
            new_ref[0] = value
            low_ref[0] = value.astype(BF16)
            update_ref[0] = update


def finish(section, me, plan, ew, sources, earlier):
    _, rows, width = ew.shape
    spec = pl.BlockSpec(
        (1, rows, width), lambda i, me, plan: (expert_at(section, me, plan, i), 0, 0)
    )
    operands, in_specs, starts = [me, plan], [], []
    low = 0
    for source in sources:
        steps, _, source_rows, _ = source.shape
        in_specs.append(
            pl.BlockSpec(
                (1, 1, source_rows, width),
                lambda i, *_, low=low, steps=steps: (jnp.clip(i - low, 0, steps - 1), 0, 0, 0),
            )
        )
        operands.append(source)
        starts.append((low, low + steps))
        low += steps
    in_specs.append(spec)
    operands.append(ew)
    aliases = {}
    if earlier is not None:
        aliases = {len(operands) + index: index for index in range(3)}
        in_specs += [pl.BlockSpec(memory_space=pl.ANY)] * 3
        operands += list(earlier)
    return pl.pallas_call(
        functools.partial(finish_kernel, section, starts),
        grid_spec=pltpu.PrefetchScalarGridSpec(
            num_scalar_prefetch=2,
            grid=(section[1],),
            in_specs=in_specs,
            out_specs=[spec] * 3,
        ),
        out_shape=[jax.ShapeDtypeStruct(ew.shape, kind) for kind in (F32, BF16, BF16)],
        input_output_aliases=aliases,
        compiler_params=pltpu.CompilerParams(vmem_limit_bytes=STREAM_LIMIT),
        name="finish",
    )(*operands)


def permute(array, pairs):
    return lax.ppermute(array, "fsdp", pairs)


def together(*arrays):
    return lax.optimization_barrier(arrays)


def far_pairs(table, step, to_owners):
    devices = table.shape[1]
    pairs = [(d ^ (2 * step), d) for d in range(devices) if table[0, d] == 1]
    return pairs if to_owners else [(there, here) for here, there in pairs]


def exchange_near(blocks, devices):
    groups = np.arange(devices).reshape(2, -1).tolist()
    return lax.all_to_all(blocks, "fsdp", 0, 0, axis_index_groups=groups, tiled=True)


def shards(expert_grad, expert_momentum, expert_master, kv_grad, kv_momentum, kv_master):
    devices = lax.axis_size("fsdp")
    chips = devices // 2
    far_steps = range(chips // 2, chips)
    me = lax.axis_index("fsdp").reshape(1)
    shape = expert_grad.shape
    rows, width = shape[2], shape[3]
    kv_rows = kv_grad.shape[1]
    flat = lambda array: array.reshape(-1, rows, width)
    eg, em, ew = flat(expert_grad), flat(expert_momentum), flat(expert_master)
    table = owner_table(eg.shape[0], kv_grad.shape[0], devices)
    sections = Plan(table)
    owns = sections.section([[device] for device in range(devices)])
    near_own = sections.section(near_owners(devices))
    far_own = sections.section(far_owners(devices, 0))
    far_other = sections.section(far_owners(devices, 1))
    plan = sections.array()
    slot = kv_slot(table)
    count = CLIP_RATIO * math.sqrt(devices * (expert_grad.size + kv_grad.size))
    cores = [(device, device ^ 1) for device in range(devices)]
    mirrors = [(device, device ^ chips) for device in range(devices)]

    total, gv, mv = load(eg, em)
    partial, staged, away = stage(
        far_other, devices, me, plan, total, gv, mv, kv_grad, kv_momentum
    )
    squares = lax.all_to_all(partial, "fsdp", 0, 0, tiled=True)
    mirror, sibling = permute(away, mirrors), permute(staged, cores)
    squares, sibling, mirror = together(squares, sibling, mirror)

    clip, *far = form_far(far_own, me, plan, squares, gv, mv, sibling, count)
    clip, far[0] = together(clip, far[0])
    near = form_near(near_own, me, plan, clip, gv, mv, kv_grad, kv_momentum, mirror)
    far = [permute(block, far_pairs(table, step, True)) for step, block in zip(far_steps, far)]
    near = exchange_near(near, devices)
    near_rows, near_gram = near_product(owns, me, plan, near, rows)

    near_rows, clip = together(near_rows, clip)
    factor = clip[0, 0]
    expert_moment_out = MOMENTUM * expert_momentum + factor * expert_grad
    kv_moment_out = MOMENTUM * kv_momentum + factor * kv_grad
    near_rows, expert_moment_out, kv_moment_out = together(
        near_rows, expert_moment_out, kv_moment_out
    )
    near, far = orthogonal_update(owns, me, plan, near, near_rows, near_gram, far, kv_rows)

    far = [permute(block, far_pairs(table, step, False)) for step, block in zip(far_steps, far)]
    near = exchange_near(near, devices)
    kv_back = permute(near[slot, kv_rows : 2 * kv_rows], mirrors)
    done = finish(near_own, me, plan, ew, [near[:, None]], None)
    far[0], *done = together(far[0], *done)
    others = permute(gather_far(far), cores)
    done = finish(far_own, me, plan, ew, [block[None] for block in far], done)
    done = finish(far_other, me, plan, ew, [others[:, None]], done)
    kv_back, eo, eb, eu = together(kv_back, *done)
    ko, kb, ku = finish_kv(me, devices, near, slot, kv_back, kv_master)
    return (
        eo.reshape(shape),
        expert_moment_out,
        eb.reshape(shape),
        eu.reshape(shape),
        ko,
        kv_moment_out,
        kb,
        ku,
    )


def solution(mesh):
    expert = P("groups", None, "fsdp", None)
    kv = P("groups", "fsdp", None)
    return jax.shard_map(
        shards,
        mesh=mesh,
        in_specs=(expert, expert, expert, kv, kv, kv),
        out_specs=(expert, expert, expert, expert, kv, kv, kv, kv),
        check_vma=False,
    )
```

time: 187 us -> 190 us (1.016)
  the two profiles are of different devices: /device:TPU:7 before, /device:TPU:1 now
where the time goes in v1:
time: 190 us; the launch traced here: 188 us
  waiting for transfers between devices  71.4 us (38%)
  starting transfers between devices  46.8 us (25%)
  Pallas kernels  34.2 us (18%)
  blocking collectives  14.6 us (8%)
  local copies, waits for them, and re-layouts  10.8 us (6%)
  other arithmetic  9.61 us (5%)
    all_to_all x2, waiting for transfers between devices, exchange_near(): lax.all_to_all(blocks, 'fsdp', 0, 0, axis_index_groups=groups, tiled=True)  61.4 us
    ppermute x12, starting transfers between devices, permute(): return lax.ppermute(array, 'fsdp', pairs)  32.6 us
    all_to_all x1, blocking collectives, shards(): squares = lax.all_to_all(partial, 'fsdp', 0, 0, tiled=True)  14.6 us
    all_to_all x2, starting transfers between devices, exchange_near(): lax.all_to_all(blocks, 'fsdp', 0, 0, axis_index_groups=groups, tiled=True)  14.2 us
    pallas_call x3, Pallas kernels, finish(): pl.pallas_call(functools.partial(finish_kernel, section, starts), grid_sp...  10.4 us
    unnamed x34, local copies, waits for them, and re-layouts  10.2 us
    pallas_call x1, Pallas kernels, orthogonal_update(): pl.pallas_call(functools.partial(transform_kernel, owns, gain, kv_rows),...  10.1 us
    ppermute x12, waiting for transfers between devices, permute(): return lax.ppermute(array, 'fsdp', pairs)  10.1 us
  transfers between devices with their start and end apart: 14, of which 4 were waited for; matrix products, arithmetic and copies ran while one was open for 5% of the time, Pallas kernels for 6%

profile of v1, /device:TPU:1, one launch (start us, length us, event | category | flops | bytes accessed | tf_op | source)
XLA Modules:
  0.0 188.3 jit_solution(2859269127913184097)
XLA Ops:
  0.7 3.9 %load.1 = (f32[8,2048]{1,0:T(8,128)S(1)}, f32[12,48,2048]{2,1,0:T(8,128)S(1)}, f32[12,48,2048]{2,1,0:T(8,128)S(1)}) custom-call(f32[12,48,2048]{2,1,0:T(8,128)} %bitcast.28, f32[12,48,2048]{2,1,0:T(8,128)} %bitcast.29), custom_call_target="tpu_custom_call" | custom-call | tf_op jit(solution)/shard_map/load/pallas_call | solution.py:125
  5.6 3.8 %collective-permute-start.1 = (bf16[2,32,2048]{2,1,0:T(8,128)(2,1)S(1)}, bf16[2,32,2048]{2,1,0:T(8,128)(2,1)S(1)}, u32[]{:S(2)}, u32[]{:S(2)}) collective-permute-start(bf16[2,32,2048]{2,1,0:T(8,128)(2,1)S(1)} %get-tuple-element.63), channel_id=1, source_target_pairs={{0,8},{1,9},{2,10},{3,11},{4,12},{5,13},{6,14},{7,15},{8,0},{9,1},... | collective-permute-start | bytes 786440 | tf_op jit(solution)/shard_map/ppermute | solution.py:530
  9.4 14.6 %all_to_all.15.squares = f32[16,8,128]{2,1,0:T(8,128)S(1)} all-to-all(f32[16,8,128]{2,1,0:T(8,128)S(1)} %get-tuple-element.61), channel_id=1, replica_groups=mesh['groups'=2,'fsdp'=16] {'fsdp'}, dimensions={0} | all-to-all | bytes 131072 | tf_op jit(solution)/shard_map/all_to_all | solution.py:574
  23.9 1.2 far.1
  28.2 1.8 form.1
  30.0 1.3 copy-done.2
  31.3 4.5 %all-to-all-start.1 = ((bf16[8,64,2048]{2,1,0:T(8,128)(2,1)}), bf16[8,64,2048]{2,1,0:T(8,128)(2,1)S(1)}, u32[]{:S(2)}, u32[]{:S(2)}) async-start(bf16[8,64,2048]{2,1,0:T(8,128)(2,1)} %copy-done.2), calls=%async_computation.1 | async-start | bytes 4194304 | tf_op jit(solution)/shard_map/all_to_all | solution.py:545
  35.8 4.5 %collective-permute-start.2 = (bf16[2,48,2048]{2,1,0:T(8,128)(2,1)}, bf16[2,48,2048]{2,1,0:T(8,128)(2,1)S(1)}, u32[]{:S(2)}, u32[]{:S(2)}) collective-permute-start(bf16[2,48,2048]{2,1,0:T(8,128)(2,1)} %copy-done.14), channel_id=1, source_target_pairs={{8,0},{9,1},{10,2},{12,4},{14,6},{15,7},{0,8},{1,9},{2,10},{4,12},... | collective-permute-start | bytes 1179656 | tf_op jit(solution)/shard_map/ppermute | solution.py:530
  40.3 1.3 collective-permute-start.3
  41.6 1.3 collective-permute-start.4
  42.9 4.0 %collective-permute-start.5 = (bf16[2,48,2048]{2,1,0:T(8,128)(2,1)}, bf16[2,48,2048]{2,1,0:T(8,128)(2,1)}, u32[]{:S(2)}, u32[]{:S(2)}) collective-permute-start(bf16[2,48,2048]{2,1,0:T(8,128)(2,1)} %copy-done.8), channel_id=1, source_target_pairs={{14,0},{15,1},{12,2},{10,4},{8,6},{9,7},{6,8},{7,9},{4,10},{2,12},... | collective-permute-start | bytes 1179656 | tf_op jit(solution)/shard_map/ppermute | solution.py:530
  46.9 28.2 %all-to-all-done.1.near = bf16[8,64,2048]{2,1,0:T(8,128)(2,1)S(1)} async-done(((bf16[8,64,2048]{2,1,0:T(8,128)(2,1)}), bf16[8,64,2048]{2,1,0:T(8,128)(2,1)S(1)}, u32[]{:S(2)}, u32[]{:S(2)}) %all-to-all-start.1) | async-done | bytes 2097184 | tf_op jit(solution)/shard_map/all_to_all | solution.py:545
  75.1 1.6 near.1
  77.2 8.1 %multiply_add_fusion = f32[4,3,48,2048]{3,2,1,0:T(8,128)} fusion(f32[4,3,48,2048]{3,2,1,0:T(8,128)} %param.7, f32[4,3,48,2048]{3,2,1,0:T(8,128)} %param.8, f32[]{:T(128)} %bitcast.3), kind=kLoop, calls=%fused_computation | loop fusion | flops 3538944 | bytes 14155780 | tf_op jit(solution)/shard_map/add | solution.py:587
  85.3 1.5 multiply_add_fusion.1
  86.8 10.1 %transform.1 = (bf16[768,2048]{1,0:T(8,128)(2,1)S(1)}, bf16[768,768]{1,0:T(8,128)(2,1)S(1)}, f32[768,128]{1,0:T(8,128)S(1)}, bf16[2,48,2048]{2,1,0:T(8,128)(2,1)...) custom-call(s32[1]{0:T(128)} %bitcast.me, ...), custom_call_target="tpu_custom_call" | custom-call | tf_op jit(solution)/shard_map/transform/pallas_call | solution.py:390
  99.2 2.1 %apply.1 = bf16[8,64,2048]{2,1,0:T(8,128)(2,1)S(1)} custom-call(s32[1]{0:T(128)} %bitcast.me, s32[544]{0:T(1024)S(1)} %copy-done.6, bf16[768,2048]{1,0:T(8,128)(2,1)S(1)} %get-tuple-element.79.x, bf16[768,768]{1,0:T(8,128)(2,1)S(1)} %get-tuple-element.80.rest, f32[768,128]{1,0:T(8,128)S(1)} %get-tuple-element.81.lead), custom_call_target="tpu_custom_call" | custom-call | tf_op jit(solution)/shard_map/apply/pallas_call | solution.py:404
  101.3 1.3 copy-done.1
  102.6 9.7 %all-to-all-start.2 = ((bf16[8,64,2048]{2,1,0:T(8,128)(2,1)}), bf16[8,64,2048]{2,1,0:T(8,128)(2,1)S(1)}, u32[]{:S(2)}, u32[]{:S(2)}) async-start(bf16[8,64,2048]{2,1,0:T(8,128)(2,1)} %copy-done.1), calls=%async_computation.2 | async-start | bytes 4194304 | tf_op jit(solution)/shard_map/all_to_all | solution.py:545
  112.4 9.4 %collective-permute-start.7 = (bf16[2,48,2048]{2,1,0:T(8,128)(2,1)}, bf16[2,48,2048]{2,1,0:T(8,128)(2,1)S(1)}, u32[]{:S(2)}, u32[]{:S(2)}) collective-permute-start(bf16[2,48,2048]{2,1,0:T(8,128)(2,1)} %copy-done.13), channel_id=1, source_target_pairs={{0,8},{1,9},{2,10},{4,12},{6,14},{7,15},{8,0},{9,1},{10,2},{12,4},... | collective-permute-start | bytes 1179656 | tf_op jit(solution)/shard_map/ppermute | solution.py:530
  121.7 1.8 collective-permute-start.8
  123.5 2.1 %collective-permute-start.9 = (bf16[2,48,2048]{2,1,0:T(8,128)(2,1)}, bf16[2,48,2048]{2,1,0:T(8,128)(2,1)}, u32[]{:S(2)}, u32[]{:S(2)}) collective-permute-start(bf16[2,48,2048]{2,1,0:T(8,128)(2,1)} %copy-done.9), channel_id=1, source_target_pairs={{0,12},{1,13},{2,14},{4,8},{6,10},{7,11},{8,4},{9,5},{10,6},{12,0}... | collective-permute-start | bytes 1179656 | tf_op jit(solution)/shard_map/ppermute | solution.py:530
  125.6 3.4 %collective-permute-start.10 = (bf16[2,48,2048]{2,1,0:T(8,128)(2,1)}, bf16[2,48,2048]{2,1,0:T(8,128)(2,1)}, u32[]{:S(2)}, u32[]{:S(2)}) collective-permute-start(bf16[2,48,2048]{2,1,0:T(8,128)(2,1)} %copy-done.7), channel_id=1, source_target_pairs={{0,14},{1,15},{2,12},{4,10},{6,8},{7,9},{8,6},{9,7},{10,4},{12,2},... | collective-permute-start | bytes 1179656 | tf_op jit(solution)/shard_map/ppermute | solution.py:530
  129.0 33.2 %all-to-all-done.2.kv = bf16[8,64,2048]{2,1,0:T(8,128)(2,1)S(1)} async-done(((bf16[8,64,2048]{2,1,0:T(8,128)(2,1)}), bf16[8,64,2048]{2,1,0:T(8,128)(2,1)S(1)}, u32[]{:S(2)}, u32[]{:S(2)}) %all-to-all-start.2) | async-done | bytes 2097184 | tf_op jit(solution)/shard_map/all_to_all | solution.py:545
  162.2 2.3 %copy-done = f32[4,3,48,2048]{3,2,1,0:T(8,128)S(1)} copy-done((f32[4,3,48,2048]{3,2,1,0:T(8,128)S(1)}, f32[4,3,48,2048]{3,2,1,0:T(8,128)}, u32[]{:S(2)}) %copy-start) | copy-done | bytes 4718616
  164.6 4.6 %finish.3 = (f32[12,48,2048]{2,1,0:T(8,128)}, bf16[12,48,2048]{2,1,0:T(8,128)(2,1)}, bf16[12,48,2048]{2,1,0:T(8,128)(2,1)}) custom-call(s32[1]{0:T(128)} %bitcast.me, s32[544]{0:T(1024)S(1)} %copy-done.6, bf16[8,1,64,2048]{3,2,1,0:T(8,128)(2,1)S(1)} %bitcast.23, f32[12,48,2048]{2,1,0:T(8,128)S(1)} %bitcast.18), custom_call_target="tpu_custom_call" | custom-call | tf_op jit(solution)/shard_map/finish/pallas_call | solution.py:514
  169.1 9.9 %collective-permute-done.10.refs_3_ = bf16[2,48,2048]{2,1,0:T(8,128)(2,1)} collective-permute-done((bf16[2,48,2048]{2,1,0:T(8,128)(2,1)}, bf16[2,48,2048]{2,1,0:T(8,128)(2,1)}, u32[]{:S(2)}, u32[]{:S(2)}) %collective-permute-start.10) | collective-permute-done | bytes 393248 | tf_op jit(solution)/shard_map/ppermute | solution.py:530
  179.1 1.2 gather.1
  180.3 0.9 collective-permute-start.11
  181.3 3.0 %finish.4 = (f32[12,48,2048]{2,1,0:T(8,128)}, bf16[12,48,2048]{2,1,0:T(8,128)(2,1)}, bf16[12,48,2048]{2,1,0:T(8,128)(2,1)}) custom-call(s32[1]{0:T(128)} %bitcast.me, s32[544]{0:T(1024)S(1)} %copy-done.6, bf16[1,2,48,2048]{3,2,1,0:T(8,128)(2,1)S(1)} %bitcast.24, ...), custom_call_target="tpu_custom_call", output_to_operand_aliasing={{0}: (7, {}), {1}: (8, {}), {2}: (9, {})} | custom-call | tf_op jit(solution)/shard_map/finish/pallas_call | solution.py:514
  184.4 2.8 %finish.5 = (f32[12,48,2048]{2,1,0:T(8,128)}, bf16[12,48,2048]{2,1,0:T(8,128)(2,1)}, bf16[12,48,2048]{2,1,0:T(8,128)(2,1)}) custom-call(s32[1]{0:T(128)} %bitcast.me, s32[544]{0:T(1024)S(1)} %copy-done.6, bf16[4,1,48,2048]{3,2,1,0:T(8,128)(2,1)S(1)} %bitcast.26, ...), custom_call_target="tpu_custom_call", output_to_operand_aliasing={{0}: (4, {}), {1}: (5, {}), {2}: (6, {})} | custom-call | tf_op jit(solution)/shard_map/finish/pallas_call | solution.py:514
  187.3 1.1 kv.1
  (48 shorter events, 7.0 us)
Async XLA Ops:
  0.6 3.9 %copy-start.3 = (f32[2,32,2048]{2,1,0:T(8,128)S(1)}, f32[2,32,2048]{2,1,0:T(8,128)}, u32[]{:S(2)}) copy-start(f32[2,32,2048]{2,1,0:T(8,128)} %kg.3) | copy-start | bytes 1572868
  0.6 4.0 %copy-start.4 = (f32[2,32,2048]{2,1,0:T(8,128)S(1)}, f32[2,32,2048]{2,1,0:T(8,128)}, u32[]{:S(2)}) copy-start(f32[2,32,2048]{2,1,0:T(8,128)} %km.3) | copy-start | bytes 1572868
  0.7 4.0 %copy-start.6 = (s32[544]{0:T(1024)S(1)}, s32[544]{0:T(1024)}, u32[]{:S(2)}) copy-start(s32[544]{0:T(1024)} %constant.2.clone.plan) | copy-start | bytes 6532
  5.5 18.5 %collective-permute-start = (bf16[2,4,48,2048]{3,2,1,0:T(8,128)(2,1)S(1)}, bf16[2,4,48,2048]{3,2,1,0:T(8,128)(2,1)S(1)}, u32[]{:S(2)}, u32[]{:S(2)}) collective-permute-start(bf16[2,4,48,2048]{3,2,1,0:T(8,128)(2,1)S(1)} %get-tuple-element.62), channel_id=1, source_target_pairs={{0,1},{1,0},{2,3},{3,2},{4,5},{5,4},{6,7},{7,6},{8,9},{9,8},{10,11... | collective-permute-start | bytes 4718600 | tf_op jit(solution)/shard_map/ppermute | solution.py:530
  5.6 18.4 %collective-permute-start.1 = (bf16[2,32,2048]{2,1,0:T(8,128)(2,1)S(1)}, bf16[2,32,2048]{2,1,0:T(8,128)(2,1)S(1)}, u32[]{:S(2)}, u32[]{:S(2)}) collective-permute-start(bf16[2,32,2048]{2,1,0:T(8,128)(2,1)S(1)} %get-tuple-element.63), channel_id=1, source_target_pairs={{0,8},{1,9},{2,10},{3,11},{4,12},{5,13},{6,14},{7,15},{8,0},{9,1},... | collective-permute-start | bytes 786440 | tf_op jit(solution)/shard_map/ppermute | solution.py:530
  25.2 0.7 copy-start.10
  25.9 0.7 copy-start.12
  26.7 0.7 copy-start.14
  27.4 0.7 copy-start.8
  30.0 1.3 copy-start.2
  31.3 43.8 %all-to-all-start.1 = ((bf16[8,64,2048]{2,1,0:T(8,128)(2,1)}), bf16[8,64,2048]{2,1,0:T(8,128)(2,1)S(1)}, u32[]{:S(2)}, u32[]{:S(2)}) async-start(bf16[8,64,2048]{2,1,0:T(8,128)(2,1)} %copy-done.2), calls=%async_computation.1 | async-start | bytes 4194304 | tf_op jit(solution)/shard_map/all_to_all | solution.py:545
  35.8 51.0 %collective-permute-start.2 = (bf16[2,48,2048]{2,1,0:T(8,128)(2,1)}, bf16[2,48,2048]{2,1,0:T(8,128)(2,1)S(1)}, u32[]{:S(2)}, u32[]{:S(2)}) collective-permute-start(bf16[2,48,2048]{2,1,0:T(8,128)(2,1)} %copy-done.14), channel_id=1, source_target_pairs={{8,0},{9,1},{10,2},{12,4},{14,6},{15,7},{0,8},{1,9},{2,10},{4,12},... | collective-permute-start | bytes 1179656 | tf_op jit(solution)/shard_map/ppermute | solution.py:530
  40.3 46.5 %collective-permute-start.3 = (bf16[2,48,2048]{2,1,0:T(8,128)(2,1)}, bf16[2,48,2048]{2,1,0:T(8,128)(2,1)}, u32[]{:S(2)}, u32[]{:S(2)}) collective-permute-start(bf16[2,48,2048]{2,1,0:T(8,128)(2,1)} %copy-done.12), channel_id=1, source_target_pairs={{10,0},{11,1},{8,2},{14,4},{12,6},{13,7},{2,8},{3,9},{0,10},{6,12}... | collective-permute-start | bytes 1179656 | tf_op jit(solution)/shard_map/ppermute | solution.py:530
  41.6 45.2 %collective-permute-start.4 = (bf16[2,48,2048]{2,1,0:T(8,128)(2,1)}, bf16[2,48,2048]{2,1,0:T(8,128)(2,1)}, u32[]{:S(2)}, u32[]{:S(2)}) collective-permute-start(bf16[2,48,2048]{2,1,0:T(8,128)(2,1)} %copy-done.10), channel_id=1, source_target_pairs={{12,0},{13,1},{14,2},{8,4},{10,6},{11,7},{4,8},{5,9},{6,10},{0,12}... | collective-permute-start | bytes 1179656 | tf_op jit(solution)/shard_map/ppermute | solution.py:530
  42.9 43.9 %collective-permute-start.5 = (bf16[2,48,2048]{2,1,0:T(8,128)(2,1)}, bf16[2,48,2048]{2,1,0:T(8,128)(2,1)}, u32[]{:S(2)}, u32[]{:S(2)}) collective-permute-start(bf16[2,48,2048]{2,1,0:T(8,128)(2,1)} %copy-done.8), channel_id=1, source_target_pairs={{14,0},{15,1},{12,2},{10,4},{8,6},{9,7},{6,8},{7,9},{4,10},{2,12},... | collective-permute-start | bytes 1179656 | tf_op jit(solution)/shard_map/ppermute | solution.py:530
  96.9 0.7 copy-start.9
  97.7 0.8 copy-start.11
  98.4 0.7 copy-start.7
  98.4 4.2 %copy-start.13 = (bf16[2,48,2048]{2,1,0:T(8,128)(2,1)}, bf16[2,48,2048]{2,1,0:T(8,128)(2,1)S(1)}, u32[]{:S(2)}) copy-start(bf16[2,48,2048]{2,1,0:T(8,128)(2,1)S(1)} %get-tuple-element.82) | copy-start | bytes 1179652
  101.3 1.3 copy-start.1
  102.6 78.7 %slice-start = ((s8[4718592]{0:T(1024)(128)(4,1)}), s8[524288]{0:T(1024)(128)(4,1)S(1)}, s32[]{:S(2)}) async-start(s8[4718592]{0:T(1024)(128)(4,1)} %bitcast.19), calls=%async_computation.3 | async-start | bytes 1048576
  102.6 59.6 %all-to-all-start.2 = ((bf16[8,64,2048]{2,1,0:T(8,128)(2,1)}), bf16[8,64,2048]{2,1,0:T(8,128)(2,1)S(1)}, u32[]{:S(2)}, u32[]{:S(2)}) async-start(bf16[8,64,2048]{2,1,0:T(8,128)(2,1)} %copy-done.1), calls=%async_computation.2 | async-start | bytes 4194304 | tf_op jit(solution)/shard_map/all_to_all | solution.py:545
  112.4 56.8 %collective-permute-start.7 = (bf16[2,48,2048]{2,1,0:T(8,128)(2,1)}, bf16[2,48,2048]{2,1,0:T(8,128)(2,1)S(1)}, u32[]{:S(2)}, u32[]{:S(2)}) collective-permute-start(bf16[2,48,2048]{2,1,0:T(8,128)(2,1)} %copy-done.13), channel_id=1, source_target_pairs={{0,8},{1,9},{2,10},{4,12},{6,14},{7,15},{8,0},{9,1},{10,2},{12,4},... | collective-permute-start | bytes 1179656 | tf_op jit(solution)/shard_map/ppermute | solution.py:530
  121.7 47.4 %collective-permute-start.8 = (bf16[2,48,2048]{2,1,0:T(8,128)(2,1)}, bf16[2,48,2048]{2,1,0:T(8,128)(2,1)S(1)}, u32[]{:S(2)}, u32[]{:S(2)}) collective-permute-start(bf16[2,48,2048]{2,1,0:T(8,128)(2,1)} %copy-done.11), channel_id=1, source_target_pairs={{0,10},{1,11},{2,8},{4,14},{6,12},{7,13},{8,2},{9,3},{10,0},{12,6}... | collective-permute-start | bytes 1179656 | tf_op jit(solution)/shard_map/ppermute | solution.py:530
  123.5 45.6 %collective-permute-start.9 = (bf16[2,48,2048]{2,1,0:T(8,128)(2,1)}, bf16[2,48,2048]{2,1,0:T(8,128)(2,1)}, u32[]{:S(2)}, u32[]{:S(2)}) collective-permute-start(bf16[2,48,2048]{2,1,0:T(8,128)(2,1)} %copy-done.9), channel_id=1, source_target_pairs={{0,12},{1,13},{2,14},{4,8},{6,10},{7,11},{8,4},{9,5},{10,6},{12,0}... | collective-permute-start | bytes 1179656 | tf_op jit(solution)/shard_map/ppermute | solution.py:530
  125.6 53.5 %collective-permute-start.10 = (bf16[2,48,2048]{2,1,0:T(8,128)(2,1)}, bf16[2,48,2048]{2,1,0:T(8,128)(2,1)}, u32[]{:S(2)}, u32[]{:S(2)}) collective-permute-start(bf16[2,48,2048]{2,1,0:T(8,128)(2,1)} %copy-done.7), channel_id=1, source_target_pairs={{0,14},{1,15},{2,12},{4,10},{6,8},{7,9},{8,6},{9,7},{10,4},{12,2},... | collective-permute-start | bytes 1179656 | tf_op jit(solution)/shard_map/ppermute | solution.py:530
  162.2 2.3 %copy-start = (f32[4,3,48,2048]{3,2,1,0:T(8,128)S(1)}, f32[4,3,48,2048]{3,2,1,0:T(8,128)}, u32[]{:S(2)}) copy-start(f32[4,3,48,2048]{3,2,1,0:T(8,128)} %param.9) | copy-start | bytes 14155780
  164.6 16.7 %slice-start.1 = ((s8[4718592]{0:T(1024)(128)(4,1)}), s8[4194304]{0:T(1024)(128)(4,1)S(1)}, s32[]{:S(2)}) async-start(s8[4718592]{0:T(1024)(128)(4,1)} %bitcast.19), calls=%async_computation.4 | async-start | bytes 8388608
  180.3 4.1 %collective-permute-start.11 = (bf16[4,48,2048]{2,1,0:T(8,128)(2,1)S(1)}, bf16[4,48,2048]{2,1,0:T(8,128)(2,1)S(1)}, u32[]{:S(2)}, u32[]{:S(2)}) collective-permute-start(bf16[4,48,2048]{2,1,0:T(8,128)(2,1)S(1)} %gather.1), channel_id=1, source_target_pairs={{0,1},{1,0},{2,3},{3,2},{4,5},{5,4},{6,7},{7,6},{8,9},{9,8},{10,11... | collective-permute-start | bytes 2359304 | tf_op jit(solution)/shard_map/ppermute | solution.py:530
  181.2 6.1 %collective-permute-start.6 = (bf16[32,2048]{1,0:T(8,128)(2,1)S(1)}, bf16[32,2048]{1,0:T(8,128)(2,1)S(1)}, u32[]{:S(2)}, u32[]{:S(2)}) collective-permute-start(bf16[32,2048]{1,0:T(8,128)(2,1)S(1)} %slice_bitcast_fusion), channel_id=1, source_target_pairs={{0,8},{1,9},{2,10},{3,11},{4,12},{5,13},{6,14},{7,15},{8,0},{9,1},... | collective-permute-start | bytes 393224 | tf_op jit(solution)/shard_map/ppermute | solution.py:530
  184.4 2.9 %copy-start.5 = (f32[2,32,2048]{2,1,0:T(8,128)S(1)}, f32[2,32,2048]{2,1,0:T(8,128)}, u32[]{:S(2)}) copy-start(f32[2,32,2048]{2,1,0:T(8,128)} %kw.1) | copy-start | bytes 1572868
